TPU v7x, 128 devices: a whole 4x4x4 slice. The times are simulated.
128 devices in a mesh: wide: 32 (over z, x, core), eight: 4 (over y).
Axes of the slice: x: 4, y: 4, z: 4, core: 2. Of those that a mesh axis runs over, the one named last changes fastest.
Arguments:
- start_vectors: bfloat16 [512, 96, 4096], P('wide', 'eight'), may hold values from -6 to 6
- conductance: float32 [512, 4096], P('wide'), may hold values from 1 to 100
- counts: int32 [512], P('wide'), may hold values from 1 to 96, as said below
- element_of: int32 [512, 8], P('wide'), may hold values from 0 to 511, as said below
- capacity: float32 [512, 512], P(('wide', 'eight')), may hold values from 0.25 to 4
- coarse_in: float32 [512, 96, 64], P(('wide', 'eight')), may hold values from -6 to 6
Outputs:
- galerkin: float32 [512, 768, 768], P(('wide', 'eight'))
- coarse_out: float32 [512, 96, 64], P(('wide', 'eight'))
Inputs may be any that keep to these rules, and one draw needn't show every extreme that they name: `counts`: some neighbourhood keeps exactly 96 basis functions. For each octant o, element_of[:, o] names every element exactly once. Element e belongs to device e // 4 in the order of wide+eight, and the 16 neighbourhoods of each index of wide name, over all their octants, exactly 1 elements of each device.
All inputs are finite; a program needn't handle non-finite values.
Results may differ from a plain program's by a relative error of at most 0.0004.
Values sent between devices are 32-bit elements; how exact they have to be, the bound alone decides.
A program may use at most 192 MiB of HBM per device.

v0:
```python
import jax
import jax.numpy as jnp
from jax import lax
from jax.sharding import PartitionSpec as P

SIDE = 16
PASSES = 6
ECELLS = 512


def stencil_weights(conductance, edge_cells):
    cubic_cells = conductance.reshape(conductance.shape[:-1] + (edge_cells, edge_cells, edge_cells))
    leading = cubic_cells.ndim - 3
    padded = jnp.pad(cubic_cells, [(0, 0)] * leading + [(1, 1)] * 3, mode="edge")
    diagonal = jnp.zeros_like(cubic_cells)
    neighbour_links = []
    strides = (edge_cells * edge_cells, edge_cells, 1)
    for direction in range(3):
        position = lax.broadcasted_iota(jnp.int32, cubic_cells.shape, leading + direction)
        for toward in (-1, 1):
            starts = [0] * leading + [1, 1, 1]
            starts[leading + direction] = 1 + toward
            limits = [
                starts[dim_index] + cubic_cells.shape[dim_index]
                for dim_index in range(cubic_cells.ndim)
            ]
            beside = lax.slice(padded, starts, limits)
            face_weight = 0.5 * (cubic_cells + beside)
            diagonal = diagonal + face_weight
            inside = (position + toward >= 0) & (position + toward < edge_cells)
            linked = jnp.where(inside, face_weight, jnp.zeros_like(face_weight))
            neighbour_links.append((toward * strides[direction], linked.reshape(conductance.shape)))
    return (diagonal.reshape(conductance.shape), neighbour_links)


def operate(field, diagonal, neighbour_links, plane_span):
    cell_total = field.shape[-1]
    padded = jnp.pad(field, [(0, 0)] * (field.ndim - 1) + [(plane_span, plane_span)])
    result = diagonal * field
    for offset, linked in neighbour_links:
        moved = lax.slice_in_dim(
            padded, plane_span + offset, plane_span + offset + cell_total, axis=field.ndim - 1
        )
        result = result - linked * moved
    return result


def hat_bump(edge_cells):
    half_side = edge_cells // 2
    along = (jnp.arange(edge_cells, dtype=jnp.float32) + 0.5) / half_side
    rising = jnp.minimum(along, 2.0 - along)
    return (rising[:, None, None] * rising[None, :, None] * rising[None, None, :]).reshape(-1)


def filtered_basis(start, conductance, live, edge_cells, sweeps):
    diagonal, neighbour_links = stencil_weights(conductance, edge_cells)
    upper_bound = 2.0 * jnp.max(diagonal, axis=-1)
    centre = (0.5625 * upper_bound)[..., None, None]
    radius = (0.4375 * upper_bound)[..., None, None]
    diagonal = diagonal[..., None, :]
    neighbour_links = [(offset, linked[..., None, :]) for offset, linked in neighbour_links]
    plane_span = edge_cells * edge_cells
    previous = start
    current = (
        operate(previous, diagonal, neighbour_links, plane_span) - centre * previous
    ) / radius
    for repeat in range(sweeps - 1):
        previous, current = (
            current,
            2.0
            * (operate(current, diagonal, neighbour_links, plane_span) - centre * current)
            / radius
            - previous,
        )
    norm_scale = lax.rsqrt(jnp.mean(current * current, axis=-1, keepdims=True) + 1e-05)
    return current * norm_scale * hat_bump(edge_cells) * live[..., None]


def octant_pieces(basis, edge_cells):
    half_side = edge_cells // 2
    leading = basis.shape[:-1]
    rank_lead = len(leading)
    cubic = basis.reshape(leading + (2, half_side, 2, half_side, 2, half_side))
    axes_order = tuple(range(rank_lead - 1)) + (
        rank_lead,
        rank_lead + 2,
        rank_lead + 4,
        rank_lead - 1,
        rank_lead + 1,
        rank_lead + 3,
        rank_lead + 5,
    )
    cubic = jnp.transpose(cubic, axes_order)
    return cubic.reshape(leading[:-1] + (8, leading[-1], half_side * half_side * half_side))


def body(start_vectors, conductance, counts, element_of, capacity, coarse_in):
    groups = lax.axis_size("eight")
    wide_count = lax.axis_size("wide")
    devices = wide_count * groups
    local_hoods, group_width, cell_total = start_vectors.shape
    per_device = local_hoods // groups
    piece_total = local_hoods * 8
    per_pair = piece_total // devices
    vectors = coarse_in.shape[2]
    slot_ids = lax.axis_index("eight") * group_width + jnp.arange(group_width, dtype=jnp.int32)
    live = (slot_ids[None, :] < counts[:, None]).astype(jnp.float32)
    basis = filtered_basis(start_vectors.astype(jnp.float32), conductance, live, SIDE, PASSES)
    pieces = octant_pieces(basis, SIDE).reshape(piece_total, group_width, ECELLS)
    owner_dev = (element_of // per_device).reshape(-1)
    local_ids = (element_of % per_device * 8 + jnp.arange(8, dtype=jnp.int32)[None, :]).reshape(-1)
    order_ids = jnp.arange(piece_total, dtype=jnp.int32)
    earlier = (owner_dev[:, None] == owner_dev[None, :]) & (order_ids[None, :] < order_ids[:, None])
    target = owner_dev * per_pair + jnp.sum(earlier.astype(jnp.int32), axis=1)
    source_of = jnp.zeros(piece_total, jnp.int32).at[target].set(order_ids)
    coarse_rows = lax.all_to_all(coarse_in, "eight", split_axis=1, concat_axis=0, tiled=True)
    basis_out = pieces[source_of].reshape(devices, per_pair, group_width, ECELLS)
    rows_out = coarse_rows[source_of // 8].reshape(devices, per_pair, group_width, vectors)
    ids_out = local_ids[source_of].reshape(devices, per_pair)
    got_basis, got_rows, got_ids = (
        lax.all_to_all(basis_out, ("wide", "eight"), split_axis=0, concat_axis=0, tiled=True),
        lax.all_to_all(rows_out, ("wide", "eight"), split_axis=0, concat_axis=0, tiled=True),
        lax.all_to_all(ids_out, ("wide", "eight"), split_axis=0, concat_axis=0, tiled=True),
    )
    from_group = (jnp.arange(devices, dtype=jnp.int32) % groups)[:, None]
    position = (got_ids * groups + from_group).reshape(-1)
    slot_of = jnp.zeros(piece_total, jnp.int32).at[position].set(order_ids)
    basis_full = got_basis.reshape(piece_total, group_width, ECELLS)[slot_of].reshape(
        per_device, 8 * groups * group_width, ECELLS
    )
    rows_full = got_rows.reshape(piece_total, group_width, vectors)[slot_of].reshape(
        per_device, 8 * groups * group_width, vectors
    )
    weighted = basis_full * capacity[:, None, :]
    galerkin = (
        jnp.einsum("erc,esc->ers", weighted, basis_full, precision=lax.Precision.HIGHEST) / ECELLS
    )
    applied = jnp.einsum("ers,esv->erv", galerkin, rows_full, precision=lax.Precision.HIGHEST)
    back_out = applied.reshape(piece_total, group_width, vectors)[position].reshape(
        devices, per_pair, group_width, vectors
    )
    returned = lax.all_to_all(back_out, ("wide", "eight"), split_axis=0, concat_axis=0, tiled=True)
    per_piece = returned.reshape(piece_total, group_width, vectors)[target].reshape(
        local_hoods, 8, group_width, vectors
    )
    summed = jnp.sum(per_piece, axis=1)
    coarse_out = lax.all_to_all(summed, "eight", split_axis=0, concat_axis=1, tiled=True)
    return (galerkin, coarse_out)


def solution(mesh):
    in_specs = (
        P("wide", "eight", None),
        P("wide", None),
        P("wide"),
        P("wide", None),
        P(("wide", "eight"), None),
        P(("wide", "eight"), None, None),
    )
    out_specs = (P(("wide", "eight"), None, None), P(("wide", "eight"), None, None))
    return jax.shard_map(body, mesh=mesh, in_specs=in_specs, out_specs=out_specs, check_vma=False)
```

profile of v0, /device:TPU:0, one launch (start us, length us, event | category | flops | bytes accessed | tf_op | source)
XLA Modules:
  0.0 437.9 jit_solution(12564861938193181899)
XLA Ops:
  0.6 1.0 copy.89
  2.5 4.5 %all-to-all-start.2 = ((f32[4,1,6144]{2,1,0:T(1,128)}), f32[4,1,6144]{2,1,0:T(1,128)S(1)}, u32[]{:S(2)}, u32[]{:S(2)}) async-start(f32[4,1,6144]{2,1,0:T(1,128)} %reshape.347), calls=%async_computation.2 | async-start | bytes 196608 | tf_op jit(solution)/shard_map/all_to_all | solution.py:116
  7.1 1.7 reshape.251
  9.8 1.1 fusion.127
  10.9 5.6 %fusion.126 = (f32[16]{0:T(128)S(1)}, f32[16,16,16,16]{3,2,1,0:T(8,128)}) fusion(f32[16,16,16,16]{3,2,1,0:T(8,128)S(1)} %reshape.251, f32[16,18,18,1]{3,2,1,0:T(8,128)S(1)} %get-tuple-element.19, f32[16,18,1,16]{3,2,1,0:T(1,128)S(1)} %get-tuple-element.24, f32[16,1,16,16]{3,2,1,0:T(8,128)S(1)} %get-tuple-element.29, ...), kind=kLoop, calls=%fused_computation.234 | loop fusion | flops 2359280 | bytes 635456 | tf_op jit(solution)/shard_map/reduce_max | solution.py:57
  16.5 5.1 %broadcast_select_fusion.1 = (f32[16,16,16,16]{3,2,1,0:T(8,128)}, f32[16,16,16,16]{3,2,1,0:T(8,128)}, f32[16,16,16,16]{3,2,1,0:T(8,128)}) fusion(pred[16]{0:T(512)(128)(4,1)S(1)} %get-tuple-element.37, f32[16,16,16,16]{3,2,1,0:T(8,128)S(1)} %reshape.251, f32[16,18,1,16]{3,2,1,0:T(1,128)S(1)} %get-tuple-element.24, ...), kind=kLoop, calls=%fused_computation.181 | loop fusion | flops 1441792 | bytes 1159712 | tf_op jit(solution)/shard_map/jit(_where)/select_n | solution.py:31
  21.6 3.9 fusion.111
  25.8 3.1 mul.491
  29.0 3.1 mul.494
  32.1 3.1 mul.497
  35.3 3.1 mul.237
  38.4 3.1 mul.240
  41.5 3.1 mul.485
  44.7 3.1 mul.488
  47.8 2.7 convert_element_type.20
  50.5 2.7 copy-done.1
  53.2 7.7 %fusion.10 = f32[16,24,4096]{2,1,0:T(8,128)S(1)} fusion(f32[16,24,4096]{2,1,0:T(8,128)S(1)} %convert_element_type.20, f32[16]{0:T(128)S(1)} %get-tuple-element.35, f32[16]{0:T(128)S(1)} %get-tuple-element.34, f32[16,4096]{1,0:T(8,128)S(1)} %mul.497, f32[16,4096]{1,0:T(8,128)S(1)} %mul.494, f32[16,4096]{1,0:T(8,128)S(1)} %mul.491, f32[16,4096]{1,0:T(8,128)S(1)} %mul.488, ...), kind=kLoop, calls=%fused_computation.55 | loop fusion | flops 25165824 | bytes 14418048 | tf_op jit(solution)/shard_map/div | solution.py:64
  60.9 8.7 %fusion.26 = f32[16,24,4096]{2,1,0:T(8,128)} fusion(f32[16,24,4096]{2,1,0:T(8,128)S(1)} %fusion.10, f32[16]{0:T(128)S(1)} %get-tuple-element.35, f32[16]{0:T(128)S(1)} %get-tuple-element.34, f32[16,4096]{1,0:T(8,128)S(1)} %mul.497, f32[16,4096]{1,0:T(8,128)S(1)} %mul.494, f32[16,4096]{1,0:T(8,128)S(1)} %mul.491, f32[16,4096]{1,0:T(8,128)S(1)} %mul.488, ...), kind=kLoop, calls=%fused_computation.71 | loop fusion | flops 29884416 | bytes 17563776 | tf_op jit(solution)/shard_map/sub | solution.py:70
  69.7 45.9 %fusion.42 = f32[16,24,4096]{2,1,0:T(8,128)} fusion(f32[16,24,4096]{2,1,0:T(8,128)} %fusion.26, f32[16]{0:T(128)S(1)} %get-tuple-element.35, f32[16]{0:T(128)S(1)} %get-tuple-element.34, f32[16,4096]{1,0:T(8,128)S(1)} %mul.497, f32[16,4096]{1,0:T(8,128)S(1)} %mul.494, f32[16,4096]{1,0:T(8,128)S(1)} %mul.491, f32[16,4096]{1,0:T(8,128)S(1)} %mul.488, ...), kind=kLoop, calls=%fused_computation.87 | loop fusion | flops 53477376 | bytes 20709504 | tf_op jit(solution)/shard_map/sub | solution.py:70
  115.6 25.3 %fusion.58 = f32[16,24,4096]{2,1,0:T(8,128)S(1)} fusion(f32[16,24,4096]{2,1,0:T(8,128)} %fusion.26, f32[16,24,4096]{2,1,0:T(8,128)} %fusion.42, f32[16]{0:T(128)S(1)} %get-tuple-element.35, f32[16]{0:T(128)S(1)} %get-tuple-element.34, f32[16,4096]{1,0:T(8,128)S(1)} %mul.497, f32[16,4096]{1,0:T(8,128)S(1)} %mul.494, f32[16,4096]{1,0:T(8,128)S(1)} %mul.491, ...), kind=kLoop, calls=%fused_computation.103 | loop fusion | flops 28311552 | bytes 20709504 | tf_op jit(solution)/shard_map/sub | solution.py:70
  140.9 7.4 %fusion.74 = f32[16,24,4096]{2,1,0:T(8,128)S(1)} fusion(f32[16,24,4096]{2,1,0:T(8,128)S(1)} %copy-done.2, f32[16,24,4096]{2,1,0:T(8,128)S(1)} %fusion.58, f32[16]{0:T(128)S(1)} %get-tuple-element.35, f32[16]{0:T(128)S(1)} %get-tuple-element.34, f32[16,4096]{1,0:T(8,128)S(1)} %mul.497, f32[16,4096]{1,0:T(8,128)S(1)} %mul.494, f32[16,4096]{1,0:T(8,128)S(1)} %mul.491, ...), kind=kLoop, calls=%fused_computation.119 | loop fusion | flops 28311552 | bytes 20709504 | tf_op jit(solution)/shard_map/sub | solution.py:70
  148.3 9.3 %multiply_reduce_fusion = (f32[16,24]{1,0:T(8,128)S(1)}, f32[16,24,4096]{2,1,0:T(8,128)}) fusion(f32[16,24,4096]{2,1,0:T(8,128)S(1)} %fusion.58, f32[16]{0:T(128)S(1)} %get-tuple-element.35, f32[16,24,4096]{2,1,0:T(8,128)S(1)} %fusion.74, f32[16]{0:T(128)S(1)} %get-tuple-element.34, f32[16,4096]{1,0:T(8,128)S(1)} %mul.497, f32[16,4096]{1,0:T(8,128)S(1)} %mul.494, ...), kind=kLoop, calls=%fused_computation.142 | loop fusion | flops 31456896 | bytes 20711040 | tf_op jit(solution)/shard_map/reduce_sum | solution.py:75
  158.1 1.0 scatter_custom_fusion
  159.4 1.2 gather_fusion.1
  161.4 11.4 %all-to-all-start.1 = ((s32[128,1,1]{2,1,0:T(1,128)}), s32[128,1,1]{2,1,0:T(1,128)S(1)}, u32[]{:S(2)}, u32[]{:S(2)}) async-start(s32[128,1,1]{2,1,0:T(1,128)} %copy.88), calls=%async_computation.1 | async-start | bytes 131072 | tf_op jit(solution)/shard_map/all_to_all | solution.py:123
  173.3 0.9 reduce.3
  175.1 1.9 reshape.349
  177.0 5.1 %all-to-all-done.1 = s32[128,1,1]{2,1,0:T(1,128)S(1)} async-done(((s32[128,1,1]{2,1,0:T(1,128)}), s32[128,1,1]{2,1,0:T(1,128)S(1)}, u32[]{:S(2)}, u32[]{:S(2)}) %all-to-all-start.1) | async-done | bytes 544 | tf_op jit(solution)/shard_map/all_to_all | solution.py:123
  182.1 4.7 %all-to-all-start.3 = ((f32[128,1,1536]{2,1,0:T(1,128)}), f32[128,1,1536]{2,1,0:T(1,128)S(1)}, u32[]{:S(2)}, u32[]{:S(2)}) async-start(f32[128,1,1536]{2,1,0:T(1,128)} %reshape.349), calls=%async_computation.3 | async-start | bytes 1572864 | tf_op jit(solution)/shard_map/all_to_all | solution.py:122
  186.8 6.9 %multiply_multiply_fusion = f32[16,24,4096]{2,1,0:T(8,128)} fusion(f32[16,24,4096]{2,1,0:T(8,128)} %get-tuple-element.15, f32[16,24]{1,0:T(8,128)S(1)} %compare_convert_fusion, f32[4096]{0:T(1024)S(1)} %mul.560, f32[16,24]{1,0:T(8,128)S(1)} %add_rsqrt_fusion), kind=kLoop, calls=%fused_computation.141 | loop fusion | flops 4718592 | bytes 12602368 | tf_op jit(solution)/shard_map/mul | solution.py:76
  193.7 17.6 %copy.82 = f32[16,24,4096]{1,2,0:T(8,128)} copy(f32[16,24,4096]{2,1,0:T(8,128)} %multiply_multiply_fusion) | data formatting | bytes 12582912 | tf_op jit(solution)/shard_map/mul | solution.py:76
  211.3 23.3 %copy.83 = f32[16,2,2,2,24,8,8,8]{4,7,6,5,3,2,1,0:T(8,128)} copy(f32[16,2,2,2,24,8,8,8]{4,7,3,6,2,5,1,0:T(8,128)} %bitcast.59) | data formatting | bytes 12582912 | tf_op jit(solution)/shard_map/transpose | solution.py:93
  234.6 23.2 %gather_fusion = f32[128,24,512]{1,2,0:T(8,128)} fusion(f32[128,24,512]{1,2,0:T(8,128)} %bitcast.61, s32[1024]{0:T(1024)S(1)} %get-tuple-element.39), kind=kCustom, calls=%fused_computation | custom fusion | bytes 12583424 | tf_op jit(solution)/shard_map/gather | solution.py:117
  257.8 19.9 %copy.86 = f32[128,1,24,512]{3,2,1,0:T(8,128)} copy(f32[128,1,24,512]{2,3,0,1:T(8,128)} %bitcast.62) | data formatting | bytes 12582912 | tf_op jit(solution)/shard_map/reshape | solution.py:117
  277.7 10.2 %all-to-all-start = ((f32[128,1,24,512]{3,2,1,0:T(8,128)}), f32[128,1,24,512]{3,2,1,0:T(8,128)}, u32[]{:S(2)}, u32[]{:S(2)}) async-start(f32[128,1,24,512]{3,2,1,0:T(8,128)} %copy.86), calls=%async_computation | async-start | bytes 12582912 | tf_op jit(solution)/shard_map/all_to_all | solution.py:121
  288.0 2.4 multiply_reduce_fusion.1
  290.3 1.2 scatter_custom_fusion.1
  291.6 2.5 reduce.4
  295.2 68.7 %all-to-all-done = f32[128,1,24,512]{3,2,1,0:T(8,128)} async-done(((f32[128,1,24,512]{3,2,1,0:T(8,128)}), f32[128,1,24,512]{3,2,1,0:T(8,128)}, u32[]{:S(2)}, u32[]{:S(2)}) %all-to-all-start) | async-done | bytes 6291488 | tf_op jit(solution)/shard_map/all_to_all | solution.py:121
  363.9 6.5 %gather_fusion.2 = f32[128,24,512]{2,1,0:T(8,128)} fusion(f32[128,24,512]{2,1,0:T(8,128)} %bitcast.6, s32[1024]{0:T(1024)S(1)} %pad_clamp_fusion.3), kind=kCustom, calls=%fused_computation.2 | custom fusion | bytes 12583424 | tf_op jit(solution)/shard_map/gather | solution.py:128
  370.4 21.5 %broadcast_multiply_fusion = f32[4,768,768]{2,1,0:T(8,128)S(1)} fusion(f32[4,768,512]{2,1,0:T(8,128)} %bitcast.60, f32[4,512]{1,0:T(4,128)S(1)} %copy-done.4), kind=kOutput, calls=%fused_computation.143 | convolution fusion | flops 14499446784 | bytes 15736832 | tf_op jit(solution)/shard_map/erc,esc->ers/dot_general | solution.py:136
  391.9 8.0 %fusion.129 = f32[4,768,64]{2,1,0:T(8,128)S(1)} fusion(f32[4,768,768]{2,1,0:T(8,128)S(1)} %broadcast_multiply_fusion, f32[4,768,64]{2,1,0:T(8,128)S(1)} %bitcast.64), kind=kOutput, calls=%fused_computation.237 | convolution fusion | flops 1811939328 | bytes 11010048 | tf_op jit(solution)/shard_map/ers,esv->erv/dot_general | solution.py:138
  400.7 1.9 reshape.351
  402.6 4.9 %all-to-all-start.4 = ((f32[128,1,1536]{2,1,0:T(1,128)}), f32[128,1,1536]{2,1,0:T(1,128)S(1)}, u32[]{:S(2)}, u32[]{:S(2)}) async-start(f32[128,1,1536]{2,1,0:T(1,128)} %reshape.351), calls=%async_computation.4 | async-start | bytes 1572864 | tf_op jit(solution)/shard_map/all_to_all | solution.py:142
  407.5 16.0 %all-to-all-done.4 = f32[128,1,1536]{2,1,0:T(1,128)S(1)} async-done(((f32[128,1,1536]{2,1,0:T(1,128)}), f32[128,1,1536]{2,1,0:T(1,128)S(1)}, u32[]{:S(2)}, u32[]{:S(2)}) %all-to-all-start.4) | async-done | bytes 786464 | tf_op jit(solution)/shard_map/all_to_all | solution.py:142
  423.5 2.5 reduce.5
  427.4 8.2 %all_to_all.60 = f32[4,1,6144]{2,1,0:T(1,128)S(1)} all-to-all(f32[4,1,6144]{2,1,0:T(1,128)S(1)} %reshape.353), channel_id=1, replica_groups=mesh['wide'=32,'eight'=4] {'eight'}, dimensions={0} | all-to-all | bytes 196608 | tf_op jit(solution)/shard_map/all_to_all | solution.py:147
  435.7 0.9 reduce.6
  (61 shorter events, 9.3 us)
Async XLA Ops:
  2.5 158.9 %all-to-all-start.2 = ((f32[4,1,6144]{2,1,0:T(1,128)}), f32[4,1,6144]{2,1,0:T(1,128)S(1)}, u32[]{:S(2)}, u32[]{:S(2)}) async-start(f32[4,1,6144]{2,1,0:T(1,128)} %reshape.347), calls=%async_computation.2 | async-start | bytes 196608 | tf_op jit(solution)/shard_map/all_to_all | solution.py:116
  21.6 4.0 copy-start.5
  50.5 2.7 copy-start.1
  53.2 7.7 %copy-start.3 = (bf16[16,24,4096]{2,1,0:T(8,128)(2,1)S(1)}, bf16[16,24,4096]{2,1,0:T(8,128)(2,1)}, u32[]{:S(2)}) copy-start(bf16[16,24,4096]{2,1,0:T(8,128)(2,1)} %param.6) | copy-start | bytes 9437188
  115.6 25.3 %copy-start.2 = (f32[16,24,4096]{2,1,0:T(8,128)S(1)}, f32[16,24,4096]{2,1,0:T(8,128)}, u32[]{:S(2)}) copy-start(f32[16,24,4096]{2,1,0:T(8,128)} %fusion.42) | copy-start | bytes 18874372
  148.3 11.0 %copy-start.6 = (s32[16]{0:T(128)S(1)}, s32[16]{0:T(128)}, u32[]{:S(2)}) copy-start(s32[16]{0:T(128)} %param.8) | copy-start | bytes 196
  161.4 20.7 %all-to-all-start.1 = ((s32[128,1,1]{2,1,0:T(1,128)}), s32[128,1,1]{2,1,0:T(1,128)S(1)}, u32[]{:S(2)}, u32[]{:S(2)}) async-start(s32[128,1,1]{2,1,0:T(1,128)} %copy.88), calls=%async_computation.1 | async-start | bytes 131072 | tf_op jit(solution)/shard_map/all_to_all | solution.py:123
  182.1 95.7 %all-to-all-start.3 = ((f32[128,1,1536]{2,1,0:T(1,128)}), f32[128,1,1536]{2,1,0:T(1,128)S(1)}, u32[]{:S(2)}, u32[]{:S(2)}) async-start(f32[128,1,1536]{2,1,0:T(1,128)} %reshape.349), calls=%async_computation.3 | async-start | bytes 1572864 | tf_op jit(solution)/shard_map/all_to_all | solution.py:122
  277.7 86.2 %all-to-all-start = ((f32[128,1,24,512]{3,2,1,0:T(8,128)}), f32[128,1,24,512]{3,2,1,0:T(8,128)}, u32[]{:S(2)}, u32[]{:S(2)}) async-start(f32[128,1,24,512]{3,2,1,0:T(8,128)} %copy.86), calls=%async_computation | async-start | bytes 12582912 | tf_op jit(solution)/shard_map/all_to_all | solution.py:121
  363.9 6.5 %copy-start.4 = (f32[4,512]{1,0:T(4,128)S(1)}, f32[4,512]{1,0:T(4,128)}, u32[]{:S(2)}) copy-start(f32[4,512]{1,0:T(4,128)} %param.10) | copy-start | bytes 24580
  391.9 8.1 %copy-start = (f32[4,768,768]{2,1,0:T(8,128)}, f32[4,768,768]{2,1,0:T(8,128)S(1)}, u32[]{:S(2)}) copy-start(f32[4,768,768]{2,1,0:T(8,128)S(1)} %broadcast_multiply_fusion) | copy-start | bytes 28311556
  402.6 20.9 %all-to-all-start.4 = ((f32[128,1,1536]{2,1,0:T(1,128)}), f32[128,1,1536]{2,1,0:T(1,128)S(1)}, u32[]{:S(2)}, u32[]{:S(2)}) async-start(f32[128,1,1536]{2,1,0:T(1,128)} %reshape.351), calls=%async_computation.4 | async-start | bytes 1572864 | tf_op jit(solution)/shard_map/all_to_all | solution.py:142
where the time goes:
time: 445 us; the launch traced here: 438 us
  other arithmetic  139 us (31%)
  local copies, waits for them, and re-layouts  134 us (30%)
  waiting for transfers between devices  89.7 us (20%)
  starting transfers between devices  35.8 us (8%)
  matrix products  29.5 us (7%)
  blocking collectives  8.23 us (2%)
    sub x4, other arithmetic, filtered_basis(): 2.0 * (operate(current, diagonal, neighbour_links, plane_span) - centre *...  87.3 us
    all_to_all x1, waiting for transfers between devices, body(): lax.all_to_all(basis_out, ('wide', 'eight'), split_axis=0, concat_axis=0,...  68.7 us
    transpose x1, local copies, waits for them, and re-layouts, octant_pieces(): cubic = jnp.transpose(cubic, axes_order)  23.3 us
    gather x1, local copies, waits for them, and re-layouts, body(): pieces[source_of].reshape(devices, per_pair, group_width, ECELLS)  23.2 us
    dot_general x1, matrix products, body(): jnp.einsum('erc,esc->ers', weighted, basis_full, precision=lax.Precision....  21.5 us
    reshape x1, local copies, waits for them, and re-layouts, body(): pieces[source_of].reshape(devices, per_pair, group_width, ECELLS)  19.9 us
    mul x6, local copies, waits for them, and re-layouts, operate(): result = result - linked * moved  18.9 us
    mul x1, local copies, waits for them, and re-layouts, filtered_basis(): return current * norm_scale * hat_bump(edge_cells) * live[..., None]  17.6 us
  transfers between devices with their start and end apart: 5, of which 3 were waited for; matrix products, arithmetic and copies ran while one was open for 58% of the time, Pallas kernels for 0%

commit v1 on v0

v1 whole, which is shorter than its diff:
```python
import functools

import jax
import jax.numpy as jnp
from jax import lax
from jax.experimental import pallas as pl
from jax.experimental.pallas import tpu as pltpu
from jax.sharding import PartitionSpec as P

SIDE = 16
PLANE = SIDE * SIDE
CELLS = SIDE * PLANE
ECELLS = 512
ROWS = 8
LANES = 128
FRONT = 8
FIELD = FRONT + CELLS + PLANE + 8
GROUP = 4
BOTH = ("wide", "eight")


def rows_of(a, extra=0, count=SIDE):
    return pl.ds(FRONT + a * PLANE + extra, count)


def clear_ends(field):
    field[pl.ds(0, FRONT)] = jnp.zeros((FRONT, LANES), jnp.float32)
    field[pl.ds(FRONT + CELLS, PLANE + 8)] = jnp.zeros((PLANE + 8, LANES), jnp.float32)


def link_weights(cond, coef, field):
    hoods = cond.shape[0]
    clear_ends(field)

    def bring(a, carry):
        plane = cond[:, pl.ds(pl.multiple_of(a * PLANE, PLANE), PLANE)]
        wide = jnp.broadcast_to(plane[:, None, :], (hoods, ROWS, PLANE)).reshape(LANES, PLANE)
        field[rows_of(a, 0, PLANE)] = wide.T
        return carry

    lax.fori_loop(0, SIDE, bring, 0)
    spot = lax.broadcasted_iota(jnp.int32, (SIDE, LANES), 0)
    ends = ((spot == 0) | (spot == SIDE - 1)).astype(jnp.float32)

    def one(a, largest):
        ahead = jnp.where(a < SIDE - 1, 0.5, 0.0)
        behind = jnp.where(a > 0, 0.5, 0.0)
        rim = 2.0 - 2.0 * (ahead + behind)
        last_b = None
        for b in range(SIDE):
            own = field[rows_of(a, b * SIDE)]
            link_a = ahead * (own + field[rows_of(a, b * SIDE + PLANE)])
            past = jnp.maximum(a - 1, 0)
            past_a = behind * (own + field[rows_of(past, b * SIDE)])
            edge = own * (ends + (rim + (1.0 if b in (0, SIDE - 1) else 0.0)))
            next_c = jnp.where(spot < SIDE - 1, 0.5 * (own + field[rows_of(a, b * SIDE + 1)]), 0.0)
            last_c = jnp.where(spot > 0, 0.5 * (own + field[rows_of(a, b * SIDE - 1)]), 0.0)
            edge += next_c + last_c
            diagonal = edge + link_a + past_a
            if b < SIDE - 1:
                link_b = 0.5 * (own + field[rows_of(a, b * SIDE + SIDE)])
                coef[1, pl.ds(a * PLANE + b * SIDE, SIDE)] = link_b
                diagonal += link_b
            if last_b is not None:
                diagonal += last_b
            last_b = link_b
            coef[0, pl.ds(a * PLANE + b * SIDE, SIDE)] = link_a
            coef[2, pl.ds(a * PLANE + b * SIDE, SIDE)] = next_c
            coef[3, pl.ds(a * PLANE + b * SIDE, SIDE)] = last_c
            coef[4, pl.ds(a * PLANE + b * SIDE, SIDE)] = edge
            largest = jnp.maximum(largest, diagonal)
        return largest

    largest = lax.fori_loop(0, SIDE, one, jnp.zeros((SIDE, LANES), jnp.float32))
    radius = 0.4375 * 2.0 * jnp.max(largest, axis=0, keepdims=True)
    scale = jnp.broadcast_to(2.0 / radius, (SIDE, LANES))

    def fit(a, carry):
        for b in range(SIDE):
            at = pl.ds(a * PLANE + b * SIDE, SIDE)
            for k in range(5):
                if k == 1 and b == SIDE - 1:
                    continue
                value = coef[k, at] * scale
                coef[k, at] = value - 18.0 / 7.0 if k == 4 else value
        return carry

    lax.fori_loop(0, SIDE, fit, 0)


def sweep(coef, now, old, flux, first=False, squares=False):
    flux[...] = jnp.zeros_like(flux)

    def one(a, total):
        last_b = None
        here = now[rows_of(a)]
        for base in range(0, SIDE, GROUP):
            results = []
            for b in range(base, base + GROUP):
                at = pl.ds(a * PLANE + b * SIDE, SIDE)
                result = coef[4, at] * here + flux[pl.ds(b * SIDE, SIDE)]
                if last_b is not None:
                    result += last_b
                across = coef[0, at] * (now[rows_of(a, b * SIDE + PLANE)] - here)
                result -= across
                result -= coef[2, at] * now[rows_of(a, b * SIDE + 1)]
                result -= coef[3, at] * now[rows_of(a, b * SIDE - 1)]
                if b < SIDE - 1:
                    ahead = now[rows_of(a, b * SIDE + SIDE)]
                    last_b = coef[1, at] * (ahead - here)
                    result -= last_b
                    here = ahead
                result = 0.5 * result if first else result - old[rows_of(a, b * SIDE)]
                results.append((b, across, result))
            for b, across, result in results:
                flux[pl.ds(b * SIDE, SIDE)] = across
                old[rows_of(a, b * SIDE)] = result
                if squares:
                    total += result * result
        return total

    return lax.fori_loop(0, SIDE, one, jnp.zeros((SIDE, LANES), jnp.float32))


def filtered_chunk(chunk, start, coef, even, odd, flux):
    hoods, width = start.shape[:2]
    clear_ends(even)
    clear_ends(odd)

    def bring(a, carry):
        plane = start[:, :, pl.ds(pl.multiple_of(a * PLANE, PLANE), PLANE)].astype(jnp.float32)
        plane = plane[:, chunk * ROWS : (chunk + 1) * ROWS].reshape(LANES, PLANE)
        even[rows_of(a, 0, PLANE)] = plane.T
        return carry

    lax.fori_loop(0, SIDE, bring, 0)
    sweep(coef, even, odd, flux, first=True)

    def two(step, carry):
        sweep(coef, odd, even, flux)
        sweep(coef, even, odd, flux)
        return carry

    lax.fori_loop(0, 2, two, 0)
    total = sweep(coef, odd, even, flux, squares=True)
    return jnp.sum(total, axis=0, keepdims=True) * (1.0 / CELLS)


def hat(at):
    return min(at + 0.5, SIDE - 0.5 - at) / (SIDE // 2)


def octant_of(field, scale, octant):
    dx, dy, dz = octant // 4, octant // 2 % 2, octant % 2
    spot = lax.broadcasted_iota(jnp.int32, (8, LANES), 0).astype(jnp.float32) + 8.0 * dz
    scale = scale * (jnp.minimum(spot + 0.5, SIDE - 0.5 - spot) * (2.0 / SIDE))
    parts = []
    for a in range(8 * dx, 8 * dx + 8):
        for b in range(8 * dy, 8 * dy + 8):
            cells = field[pl.ds(FRONT + a * PLANE + b * SIDE + 8 * dz, 8)]
            parts.append(cells * (scale * (hat(a) * hat(b))))
    return jnp.concatenate(parts, axis=0).T


def filter_kernel(chunk, with_rows, dest, live, start, cond, *rest):
    if with_rows:
        rows, out, rows_out, coef, even, odd, flux = rest
    else:
        out, coef, even, odd, flux = rest
    hoods = start.shape[0]
    link_weights(cond, coef, even)
    mean = filtered_chunk(chunk, start, coef, even, odd, flux)
    scale = jnp.broadcast_to(lax.rsqrt(mean + 1e-05) * live[chunk : chunk + 1], (8, LANES))
    for octant in range(8):
        turned = octant_of(even, scale, octant)
        for n in range(hoods):
            out[dest[n * 8 + octant]] = turned[n * ROWS : (n + 1) * ROWS]
    if with_rows:
        for n in range(hoods):
            for octant in range(8):
                rows_out[dest[n * 8 + octant]] = rows[n]


def filtered(chunk, dest, live, start, cond, rows=None):
    hoods = start.shape[0]
    with_rows = rows is not None
    vmem = pl.BlockSpec(memory_space=pltpu.VMEM)
    out_shape = [jax.ShapeDtypeStruct((hoods * 8, ROWS, ECELLS), jnp.float32)]
    operands = [live, start, cond]
    if with_rows:
        out_shape.append(jax.ShapeDtypeStruct((hoods * 8,) + rows.shape[1:], jnp.float32))
        operands.append(rows)
    return pl.pallas_call(
        functools.partial(filter_kernel, chunk, with_rows),
        in_specs=[pl.BlockSpec(memory_space=pltpu.SMEM)] + [vmem] * len(operands),
        out_specs=[vmem] * len(out_shape),
        scratch_shapes=[
            pltpu.VMEM((5, CELLS, LANES), jnp.float32),
            pltpu.VMEM((FIELD, LANES), jnp.float32),
            pltpu.VMEM((FIELD, LANES), jnp.float32),
            pltpu.VMEM((PLANE, LANES), jnp.float32),
        ],
        out_shape=out_shape,
        compiler_params=pltpu.CompilerParams(vmem_limit_bytes=48 * 2**20),
        cost_estimate=pl.CostEstimate(
            flops=hoods * ROWS * CELLS * 120, bytes_accessed=6 * 2**20, transcendentals=0
        ),
        name="filter",
    )(dest, *operands)


def split(wide_value):
    high = wide_value.astype(jnp.bfloat16)
    return high, (wide_value - high.astype(jnp.float32)).astype(jnp.bfloat16)


def thrice(left, right, dims):
    dot = functools.partial(
        lax.dot_general, dimension_numbers=(dims, ((), ())), preferred_element_type=jnp.float32
    )
    (lh, ll), (rh, rl) = left, right
    return dot(lh, rh) + (dot(lh, rl) + dot(ll, rh))


def element_kernel(where, weight, *rest):
    pieces, rows = rest[:24], rest[24:32]
    out, back, high, low, vec_high, vec_low = rest[32:]
    element = pl.program_id(0)
    root = jnp.sqrt(weight[0]) * (1.0 / ECELLS) ** 0.5
    for o in range(8):
        parts = [pieces[o * 3 + ch][0, g] for g in range(4) for ch in range(3)]
        whole = jnp.concatenate(parts, axis=0) * root
        high[pl.ds(o * 96, 96)], low[pl.ds(o * 96, 96)] = split(whole)
        packed = rows[o][0]
        packed = jnp.concatenate([packed[g] for g in range(3)], axis=0)
        vec = jnp.concatenate([packed[:, :64], packed[:, 64:]], axis=0)
        vec_high[pl.ds(o * 96, 96)], vec_low[pl.ds(o * 96, 96)] = split(vec)

    def block(i):
        return pl.ds(i * 256, 256)

    for i in range(3):
        for j in range(i, 3):
            product = thrice(
                (high[block(i)], low[block(i)]), (high[block(j)], low[block(j)]), ((1,), (1,))
            )
            out[0, block(i), block(j)] = product
            if i != j:
                out[0, block(j), block(i)] = product.T
    vec = (vec_high[...], vec_low[...])
    for i in range(8):
        applied = thrice(split(out[0, pl.ds(i * 96, 96)]), vec, ((1,), (0,)))
        packed = jnp.concatenate([applied[:48], applied[48:]], axis=1)
        source = where[element * 8 + i]
        for g in range(3):
            back[source, g] = packed[g * 16 : (g + 1) * 16]
        back[source, 3] = jnp.zeros((16, LANES), jnp.float32)


def elements(where, weight, got, rows):
    count = weight.shape[0]
    sources = got[0].shape[0]

    def piece(o):
        return pl.BlockSpec((1, 4, ROWS, ECELLS), lambda e, where: (where[e * 8 + o], 0, 0, 0))

    def vecs(o):
        return pl.BlockSpec((1, 4, 16, LANES), lambda e, where: (where[e * 8 + o], 0, 0, 0))

    return pl.pallas_call(
        element_kernel,
        grid_spec=pltpu.PrefetchScalarGridSpec(
            num_scalar_prefetch=1,
            grid=(count,),
            in_specs=[pl.BlockSpec((1, 1, ECELLS), lambda e, where: (e, 0, 0))]
            + [piece(o) for o in range(8) for _ in range(3)]
            + [vecs(o) for o in range(8)],
            out_specs=[
                pl.BlockSpec((1, 768, 768), lambda e, where: (e, 0, 0)),
                pl.BlockSpec((sources, 4, 16, LANES), lambda e, where: (0, 0, 0, 0)),
            ],
            scratch_shapes=[
                pltpu.VMEM((768, ECELLS), jnp.bfloat16),
                pltpu.VMEM((768, ECELLS), jnp.bfloat16),
                pltpu.VMEM((768, 64), jnp.bfloat16),
                pltpu.VMEM((768, 64), jnp.bfloat16),
            ],
        ),
        out_shape=[
            jax.ShapeDtypeStruct((count, 768, 768), jnp.float32),
            jax.ShapeDtypeStruct((sources, 4, 16, LANES), jnp.float32),
        ],
        compiler_params=pltpu.CompilerParams(vmem_limit_bytes=48 * 2**20),
        name="elements",
    )(where, weight, *[got[ch] for _ in range(8) for ch in range(3)], *[rows] * 8)


def sum_kernel(dest, back, out):
    hoods = out.shape[0]
    for n in range(hoods):
        total = back[dest[n * 8]]
        for o in range(1, 8):
            total += back[dest[n * 8 + o]]
        out[n] = total


def summed(dest, back):
    hoods = dest.shape[0] // 8
    return pl.pallas_call(
        sum_kernel,
        in_specs=[pl.BlockSpec(memory_space=pltpu.SMEM), pl.BlockSpec(memory_space=pltpu.VMEM)],
        out_specs=pl.BlockSpec(memory_space=pltpu.VMEM),
        out_shape=jax.ShapeDtypeStruct((hoods,) + back.shape[1:], jnp.float32),
        name="sums",
    )(dest, back)


def body(start_vectors, conductance, counts, element_of, capacity, coarse_in):
    me = lax.axis_index("wide") * 4 + lax.axis_index("eight")
    group = lax.axis_index("eight")
    hoods = start_vectors.shape[0]
    count = capacity.shape[0]
    dest = (element_of // count).reshape(-1)
    everyone = lax.all_gather(element_of, "wide")
    names = me * count + jnp.arange(count, dtype=jnp.int32)
    hits = everyone[None] == names[:, None, None, None]
    indices = jnp.arange(everyone.shape[0], dtype=jnp.int32)[None, :, None, None]
    where = jnp.sum(jnp.where(hits, indices, 0), axis=(1, 2)).reshape(-1)

    packed = jnp.concatenate([coarse_in[:, :48], coarse_in[:, 48:]], axis=2)
    packed = lax.all_gather(packed, "eight", tiled=True)
    rows = lax.dynamic_slice_in_dim(packed, jnp.minimum(group, 2) * 16, 16, axis=1)

    slots = group * 24 + jnp.arange(24, dtype=jnp.int32).reshape(3, 1, ROWS)
    live = (slots < counts[None, :, None]).astype(jnp.float32).reshape(3, LANES)
    send = functools.partial(lax.all_to_all, axis_name=BOTH, split_axis=0, concat_axis=0, tiled=True)
    got = []
    rows_out = None
    for chunk in range(3):
        out = filtered(
            chunk, dest, live, start_vectors, conductance, rows if chunk == 2 else None
        )
        if chunk == 2:
            rows_out = out[1]
        got.append(send(out[0]).reshape(-1, 4, ROWS, ECELLS))
    got_rows = send(rows_out).reshape(-1, 4, 16, LANES)

    weight = capacity.reshape(count, 1, ECELLS)
    galerkin, back = elements(where, weight, got, got_rows)
    back = send(back.reshape(-1, 16, LANES))
    sums = summed(dest, back)
    mine = lax.all_to_all(sums, "eight", split_axis=0, concat_axis=0, tiled=True)
    mine = mine.reshape(4, hoods // 4, 16, LANES)[:3].transpose(1, 0, 2, 3).reshape(hoods // 4, 48, LANES)
    coarse_out = jnp.concatenate([mine[:, :, :64], mine[:, :, 64:]], axis=1)
    return (galerkin, coarse_out)


def solution(mesh):
    in_specs = (
        P("wide", "eight", None),
        P("wide", None),
        P("wide"),
        P("wide", None),
        P(BOTH, None),
        P(BOTH, None, None),
    )
    out_specs = (P(BOTH, None, None), P(BOTH, None, None))
    return jax.shard_map(body, mesh=mesh, in_specs=in_specs, out_specs=out_specs, check_vma=False)
```

time: 445 us -> 241 us (0.54); the launches traced: 438 us -> 240 us
  other arithmetic: 139 us -> 1.1 us
  local copies, waits for them, and re-layouts: 134 us -> 9.83 us
  blocking collectives: 8.23 us -> 126 us
  waiting for transfers between devices: 89.7 us -> 10.7 us
  Pallas kernels: 0 us -> 65.2 us
  matrix products: 29.5 us -> 0 us
  starting transfers between devices: 35.8 us -> 26.9 us
    sub x4 -> x0, other arithmetic: 87.3 us -> none  [filtered_basis(): 2.0 * (operate(current, diagonal, neighbour_links, plane_span) - centre *...]
    all_to_all x5 -> x3, waiting for transfers between devices: 89.7 us -> 10.7 us  [the longest x2 10.7 us: body(): got.append(send(out[0]).reshape(-1, 4, ROWS, ECELLS))]
    pallas_call x0 -> x5, Pallas kernels: none -> 65.2 us  [the longest x3 50.1 us: filtered(): pl.pallas_call(functools.partial(filter_kernel, chunk, with_rows), in_spe...]
    all_to_all x1 -> x3, blocking collectives: 8.23 us -> 69.6 us  [the longest x1 34.7 us: body(): got.append(send(out[0]).reshape(-1, 4, ROWS, ECELLS))]
    all_gather x0 -> x2, blocking collectives: none -> 56 us  [the longest x1 42.9 us: body(): everyone = lax.all_gather(element_of, 'wide')]
    mul x9 -> x0, local copies, waits for them, and re-layouts: 39.7 us -> none  [the longest x6 18.9 us: operate(): result = result - linked * moved]
    gather x7 -> x0, local copies, waits for them, and re-layouts: 34 us -> none  [the longest x1 23.2 us: body(): pieces[source_of].reshape(devices, per_pair, group_width, ECELLS)]
    dot_general x2 -> x0, matrix products: 29.5 us -> none  [the longest x1 21.5 us: body(): jnp.einsum('erc,esc->ers', weighted, basis_full, precision=lax.Precision....]
  transfers between devices with their start and end apart: 5 -> 3, of which waited for: 3 -> 1; matrix products, arithmetic and copies ran while one was open for 58% -> 0% of each run, Pallas kernels for 0% -> 13%
where the time goes in v1:
time: 241 us; the launch traced here: 240 us
  blocking collectives  126 us (52%)
  Pallas kernels  65.2 us (27%)
  starting transfers between devices  26.9 us (11%)
  waiting for transfers between devices  10.7 us (4%)
  local copies, waits for them, and re-layouts  9.83 us (4%)
    pallas_call x3, Pallas kernels, filtered(): pl.pallas_call(functools.partial(filter_kernel, chunk, with_rows), in_spe...  50.1 us
    all_gather x1, blocking collectives, body(): everyone = lax.all_gather(element_of, 'wide')  42.9 us
    all_to_all x1, blocking collectives, body(): got.append(send(out[0]).reshape(-1, 4, ROWS, ECELLS))  34.7 us
    all_to_all x1, blocking collectives, body(): back = send(back.reshape(-1, 16, LANES))  25.7 us
    all_to_all x2, starting transfers between devices, body(): got.append(send(out[0]).reshape(-1, 4, ROWS, ECELLS))  16.2 us
    all_gather x1, blocking collectives, body(): packed = lax.all_gather(packed, 'eight', tiled=True)  13.1 us
    pallas_call x1, Pallas kernels, elements(): pl.pallas_call(element_kernel, grid_spec=pltpu.PrefetchScalarGridSpec(num...  13.1 us
    all_to_all x1, starting transfers between devices, body(): got_rows = send(rows_out).reshape(-1, 4, 16, LANES)  10.8 us
  transfers between devices with their start and end apart: 3, of which 1 were waited for; matrix products, arithmetic and copies ran while one was open for 0% of the time, Pallas kernels for 13%

profile of v1, /device:TPU:0, one launch (start us, length us, event | category | flops | bytes accessed | tf_op | source)
XLA Modules:
  0.0 240.3 jit_solution(15743043358198275487)
XLA Ops:
  0.6 0.0 copy-start.3
  0.7 0.7 add_select_fusion
  1.4 0.1 copy.26
  1.5 0.1 reshape.66.dest
  1.6 0.0 copy-start.5
  1.6 0.7 lt.25
  2.3 0.1 lt.26
  2.4 0.1 lt.24
  2.5 1.1 fusion.2
  3.6 0.1 copy.31
  3.7 0.1 copy.32
  3.8 0.1 pad_maximum_fusion.1
  3.9 13.1 %all_gather.11 = f32[16,48,128]{2,1,0:T(8,128)S(1)} all-gather(f32[4,48,128]{2,1,0:T(8,128)S(1)} %pad_maximum_fusion.1), channel_id=1, replica_groups=mesh['wide'=32,'eight'=4] {'eight'}, dimensions={0}, use_global_device_ids=true | all-gather | bytes 491520 | tf_op jit(solution)/shard_map/all_gather | solution.py:331
  17.0 0.0 copy-done.3
  17.0 17.8 %filter.5 = (f32[128,8,512]{2,1,0:T(8,128)S(1)}, f32[128,16,128]{2,1,0:T(8,128)}) custom-call(s32[128]{0:T(128)S(1)} %reshape.66.dest, f32[3,128]{1,0:T(4,128)S(1)} %compare_convert_fusion.live, bf16[16,24,4096]{2,1,0:T(8,128)(2,1)} %start.5, f32[16,4096]{1,0:T(8,128)S(1)} %copy-done.3, f32[16,16,128]{2,1,0:T(8,128)S(1)} %constant_dynamic-slice_fusion.rest_0_), custom_call_target="tpu_custom_call" | custom-call | flops 62914560 | bytes 6291456 | tf_op jit(solution)/shard_map/filter/pallas_call | solution.py:193
  34.8 0.0 copy-start.4
  34.8 1.3 copy-done.4
  36.1 10.8 %all-to-all-start.3 = ((f32[128,16,128]{2,1,0:T(8,128)}), f32[128,16,128]{2,1,0:T(8,128)S(1)}, u32[]{:S(2)}, u32[]{:S(2)}) async-start(f32[128,16,128]{2,1,0:T(8,128)} %get-tuple-element.7), calls=%async_computation.3 | async-start | bytes 2097152 | tf_op jit(solution)/shard_map/all_to_all | solution.py:346
  46.9 0.0 copy-start
  46.9 1.9 copy-done
  48.8 16.8 %filter.4 = f32[128,8,512]{2,1,0:T(8,128)} custom-call(s32[128]{0:T(128)S(1)} %reshape.66.dest, f32[3,128]{1,0:T(4,128)S(1)} %compare_convert_fusion.live, bf16[16,24,4096]{2,1,0:T(8,128)(2,1)S(1)} %copy-done, f32[16,4096]{1,0:T(8,128)S(1)} %copy-done.3), custom_call_target="tpu_custom_call" | custom-call | flops 62914560 | bytes 6291456 | tf_op jit(solution)/shard_map/filter/pallas_call | solution.py:193
  65.6 0.0 all-to-all-done.3
  65.7 10.3 %all-to-all-start.1 = ((f32[128,8,512]{2,1,0:T(8,128)}), f32[128,8,512]{2,1,0:T(8,128)}, u32[]{:S(2)}, u32[]{:S(2)}) async-start(f32[128,8,512]{2,1,0:T(8,128)} %filter.4), calls=%async_computation.1 | async-start | bytes 4194304 | tf_op jit(solution)/shard_map/all_to_all | solution.py:345
  75.9 0.0 copy-done.5
  75.9 0.0 copy-start.1
  75.9 1.9 copy-done.1
  77.8 15.5 %filter.3 = f32[128,8,512]{2,1,0:T(8,128)S(1)} custom-call(s32[128]{0:T(128)S(1)} %reshape.66.dest, f32[3,128]{1,0:T(4,128)S(1)} %compare_convert_fusion.live, bf16[16,24,4096]{2,1,0:T(8,128)(2,1)S(1)} %copy-done.1, f32[16,4096]{1,0:T(8,128)S(1)} %copy-done.3), custom_call_target="tpu_custom_call" | custom-call | flops 62914560 | bytes 6291456 | tf_op jit(solution)/shard_map/filter/pallas_call | solution.py:193
  93.3 0.0 copy-start.2
  93.3 1.3 copy-done.2
  94.6 10.7 %all-to-all-done.1 = f32[128,8,512]{2,1,0:T(8,128)} async-done(((f32[128,8,512]{2,1,0:T(8,128)}), f32[128,8,512]{2,1,0:T(8,128)}, u32[]{:S(2)}, u32[]{:S(2)}) %all-to-all-start.1) | async-done | bytes 2097184 | tf_op jit(solution)/shard_map/all_to_all | solution.py:345
  105.3 34.7 %all_to_all.30 = f32[128,8,512]{2,1,0:T(8,128)S(1)} all-to-all(f32[128,8,512]{2,1,0:T(8,128)} %copy-done.2), channel_id=1, replica_groups=mesh['wide'=32,'eight'=4] {'wide','eight'}, dimensions={0} | all-to-all | bytes 4194304 | tf_op jit(solution)/shard_map/all_to_all | solution.py:345
  140.0 0.0 copy-start.7
  140.0 0.0 copy-start.6
  140.0 5.9 %all-to-all-start.2 = ((f32[128,8,512]{2,1,0:T(8,128)}), f32[128,8,512]{2,1,0:T(8,128)}, u32[]{:S(2)}, u32[]{:S(2)}) async-start(f32[128,8,512]{2,1,0:T(8,128)} %copy-done.4), calls=%async_computation.2 | async-start | bytes 4194304 | tf_op jit(solution)/shard_map/all_to_all | solution.py:345
  145.9 0.0 copy-done.7
  146.0 0.0 copy-done.6
  146.0 42.9 %all-gather.1 = s32[32,16,8]{1,2,0:T(8,128)S(1)} all-gather(s32[1,16,8]{1,2,0:T(8,128)S(1)} %bitcast.29), channel_id=2, replica_groups=mesh['wide'=32,'eight'=4] {'wide'}, dimensions={0}, use_global_device_ids=true | all-gather | bytes 16896 | tf_op jit(solution)/shard_map/all_gather | solution.py:324
  188.9 0.1 copy.25
  189.0 0.2 select_reduce_fusion
  189.3 0.1 reshape.64.where
  189.3 0.0 all-to-all-done.2
  189.3 13.1 %elements.1 = (f32[4,768,768]{2,1,0:T(8,128)}, f32[32,4,16,128]{3,2,1,0:T(8,128)S(1)}) custom-call(s32[32]{0:T(128)S(1)} %reshape.64.where, f32[4,1,512]{2,1,0:T(1,128)S(1)} %reshape.65.weight, f32[32,4,8,512]{3,2,1,0:T(8,128)S(1)} %bitcast.10, f32[32,4,8,512]{3,2,1,0:T(8,128)} %bitcast.2.rest_1_.rest_4_.rest_7_.rest_10_.rest_13_.rest_16_.rest_19_.rest_22_, ...), custom_call_target="tpu_custom_call" | custom-call | tf_op jit(solution)/shard_map/elements/pallas_call | solution.py:270
  202.5 25.7 %all_to_all.31.back = f32[128,16,128]{2,1,0:T(8,128)} all-to-all(f32[128,16,128]{2,1,0:T(8,128)S(1)} %bitcast.26), channel_id=1, replica_groups=mesh['wide'=32,'eight'=4] {'wide','eight'}, dimensions={0} | all-to-all | bytes 2097152 | tf_op jit(solution)/shard_map/all_to_all | solution.py:350
  228.1 2.0 sums.1
  230.1 9.3 %all_to_all.32 = f32[16,16,128]{2,1,0:T(8,128)S(1)} all-to-all(f32[16,16,128]{2,1,0:T(8,128)} %sums.1), channel_id=1, replica_groups=mesh['wide'=32,'eight'=4] {'eight'}, dimensions={0} | all-to-all | bytes 262144 | tf_op jit(solution)/shard_map/all_to_all | solution.py:352
  239.4 0.1 fusion.3
  239.5 0.8 copy.30
  (9 shorter events, 0.1 us)
Async XLA Ops:
  0.6 16.4 %copy-start.3 = (f32[16,4096]{1,0:T(8,128)S(1)}, f32[16,4096]{1,0:T(8,128)}, u32[]{:S(2)}) copy-start(f32[16,4096]{1,0:T(8,128)} %cond.5) | copy-start | bytes 786436
  1.6 74.4 %copy-start.5 = (s32[128]{0:T(128)}, s32[128]{0:T(128)S(1)}, u32[]{:S(2)}) copy-start(s32[128]{0:T(128)S(1)} %reshape.66.dest) | copy-start | bytes 1540
  34.8 1.3 copy-start.4
  36.1 29.5 %all-to-all-start.3 = ((f32[128,16,128]{2,1,0:T(8,128)}), f32[128,16,128]{2,1,0:T(8,128)S(1)}, u32[]{:S(2)}, u32[]{:S(2)}) async-start(f32[128,16,128]{2,1,0:T(8,128)} %get-tuple-element.7), calls=%async_computation.3 | async-start | bytes 2097152 | tf_op jit(solution)/shard_map/all_to_all | solution.py:346
  46.9 1.9 copy-start
  65.7 39.6 %all-to-all-start.1 = ((f32[128,8,512]{2,1,0:T(8,128)}), f32[128,8,512]{2,1,0:T(8,128)}, u32[]{:S(2)}, u32[]{:S(2)}) async-start(f32[128,8,512]{2,1,0:T(8,128)} %filter.4), calls=%async_computation.1 | async-start | bytes 4194304 | tf_op jit(solution)/shard_map/all_to_all | solution.py:345
  75.9 1.9 copy-start.1
  93.3 1.3 copy-start.2
  140.0 5.9 %copy-start.7 = (f32[4,512]{1,0:T(4,128)S(1)}, f32[4,512]{1,0:T(4,128)}, u32[]{:S(2)}) copy-start(f32[4,512]{1,0:T(4,128)} %param.10) | copy-start | bytes 24580
  140.0 6.0 %copy-start.6 = (s32[16,8]{0,1:T(8,128)S(1)}, s32[16,8]{0,1:T(8,128)}, u32[]{:S(2)}) copy-start(s32[16,8]{0,1:T(8,128)} %param.9) | copy-start | bytes 1540
  140.0 49.3 %all-to-all-start.2 = ((f32[128,8,512]{2,1,0:T(8,128)}), f32[128,8,512]{2,1,0:T(8,128)}, u32[]{:S(2)}, u32[]{:S(2)}) async-start(f32[128,8,512]{2,1,0:T(8,128)} %copy-done.4), calls=%async_computation.2 | async-start | bytes 4194304 | tf_op jit(solution)/shard_map/all_to_all | solution.py:345

commit v2 on v1

--- a/solution.py
+++ b/solution.py
@@ -17,6 +17,7 @@
 FIELD = FRONT + CELLS + PLANE + 8
 GROUP = 4
 BOTH = ("wide", "eight")
+MESH = pl.DeviceIdType.MESH
 
 
 def rows_of(a, extra=0, count=SIDE):
@@ -162,51 +163,148 @@
     return jnp.concatenate(parts, axis=0).T
 
 
-def filter_kernel(chunk, with_rows, dest, live, start, cond, *rest):
-    if with_rows:
-        rows, out, rows_out, coef, even, odd, flux = rest
-    else:
-        out, coef, even, odd, flux = rest
+def partner(k, wide, eight):
+    z, x, core = wide // 8, wide // 2 % 4, wide % 2
+    z = (z + k // 16 + 2 * (k // 4) + 3 * k) % 4
+    x = (x + k // 4 + k) % 4
+    core = (core + k // 64 + k) % 2
+    return (z * 4 + x) * 2 + core, (eight + k) % 4
+
+
+def all_of(ref):
+    return lambda sem: pltpu.make_async_copy(ref, ref, sem)
+
+
+def exchange_kernel(
+    order, live, start, cond, coarse, ids,
+    got, got_rows, table,
+    coef, even, odd, flux, pieces, outgoing, coarse_rows, outgoing_rows,
+    send_sem, recv_sem, own_sem,
+):
+    wide, eight = lax.axis_index("wide"), lax.axis_index("eight")
+    groups, wides = lax.axis_size("eight"), lax.axis_size("wide")
+    devices = groups * wides
+    me = wide * groups + eight
     hoods = start.shape[0]
+    mine = coarse.shape[0]
+
+    for n in range(mine):
+        packed = jnp.concatenate([coarse[n, :48], coarse[n, 48:]], axis=1)
+        coarse_rows[pl.ds(eight * mine + n, 1)] = packed[None]
+    own_rows = coarse_rows.at[pl.ds(eight * mine, mine)]
+    for k in range(1, groups):
+        pltpu.make_async_remote_copy(
+            src_ref=own_rows, dst_ref=own_rows, send_sem=send_sem.at[3], recv_sem=recv_sem.at[3],
+            device_id=(wide, (eight + k) % groups), device_id_type=MESH,
+        ).start()
+
+    def tell(k, carry):
+        pltpu.make_async_remote_copy(
+            src_ref=ids, dst_ref=table.at[wide], send_sem=send_sem.at[4], recv_sem=recv_sem.at[4],
+            device_id=((wide + k) % wides, eight), device_id_type=MESH,
+        ).start()
+        return carry
+
+    lax.fori_loop(1, wides, tell, 0)
+    own_ids = pltpu.make_async_copy(ids, table.at[wide], own_sem.at[4])
+    own_ids.start()
+
     link_weights(cond, coef, even)
-    mean = filtered_chunk(chunk, start, coef, even, odd, flux)
-    scale = jnp.broadcast_to(lax.rsqrt(mean + 1e-05) * live[chunk : chunk + 1], (8, LANES))
-    for octant in range(8):
-        turned = octant_of(even, scale, octant)
-        for n in range(hoods):
-            out[dest[n * 8 + octant]] = turned[n * ROWS : (n + 1) * ROWS]
-    if with_rows:
-        for n in range(hoods):
-            for octant in range(8):
-                rows_out[dest[n * 8 + octant]] = rows[n]
-
-
-def filtered(chunk, dest, live, start, cond, rows=None):
+
+    three = coarse_rows.at[pl.ds(0, mine * (groups - 1))]
+    all_of(three)(recv_sem.at[3]).wait()
+
+    first = jnp.minimum(eight, 2) * 16
+
+    def take_rows(to):
+        outgoing_rows[pl.ds(to, 1)] = coarse_rows[pl.ds(order[to] // 8, 1), pl.ds(first, 16)]
+
+    def send_rows(k, carry):
+        to_wide, to_eight = partner(k, wide, eight)
+        to = to_wide * groups + to_eight
+        take_rows(to)
+        pltpu.make_async_remote_copy(
+            src_ref=outgoing_rows.at[to], dst_ref=got_rows.at[me], send_sem=send_sem.at[5],
+            recv_sem=recv_sem.at[5], device_id=(to_wide, to_eight), device_id_type=MESH,
+        ).start()
+        return carry
+
+    lax.fori_loop(1, devices, send_rows, 0)
+    take_rows(me)
+    kept_rows = pltpu.make_async_copy(outgoing_rows.at[me], got_rows.at[me], own_sem.at[5])
+    kept_rows.start()
+    kept = []
+    for chunk in range(3):
+        mean = filtered_chunk(chunk, start, coef, even, odd, flux)
+        scale = jnp.broadcast_to(lax.rsqrt(mean + 1e-05) * live[chunk : chunk + 1], (8, LANES))
+        for octant in range(8):
+            turned = octant_of(even, scale, octant)
+            for n in range(hoods):
+                pieces[n * 8 + octant] = turned[n * ROWS : (n + 1) * ROWS]
+
+        def send(k, carry):
+            to_wide, to_eight = partner(k, wide, eight)
+            to = to_wide * groups + to_eight
+            outgoing[chunk, pl.ds(to, 1)] = pieces[pl.ds(order[to], 1)]
+            pltpu.make_async_remote_copy(
+                src_ref=outgoing.at[chunk, to], dst_ref=got.at[chunk, me], send_sem=send_sem.at[chunk],
+                recv_sem=recv_sem.at[chunk], device_id=(to_wide, to_eight), device_id_type=MESH,
+            ).start()
+            return carry
+
+        lax.fori_loop(1, devices, send, 0)
+        outgoing[chunk, pl.ds(me, 1)] = pieces[pl.ds(order[me], 1)]
+        kept.append(pltpu.make_async_copy(outgoing.at[chunk, me], got.at[chunk, me], own_sem.at[chunk]))
+        kept[-1].start()
+
+    own_ids.wait()
+    kept_rows.wait()
+    all_of(three)(send_sem.at[3]).wait()
+    others = table.at[pl.ds(0, wides - 1)]
+    all_of(others)(send_sem.at[4]).wait()
+    all_of(others)(recv_sem.at[4]).wait()
+    others = got_rows.at[pl.ds(0, devices - 1)]
+    all_of(others)(send_sem.at[5]).wait()
+    all_of(others)(recv_sem.at[5]).wait()
+    for chunk in range(3):
+        kept[chunk].wait()
+        others = got.at[chunk, pl.ds(0, devices - 1)]
+        all_of(others)(send_sem.at[chunk]).wait()
+        all_of(others)(recv_sem.at[chunk]).wait()
+
+
+def exchanged(order, live, start, cond, coarse, ids):
     hoods = start.shape[0]
-    with_rows = rows is not None
+    pieces = hoods * 8
+    wides = lax.axis_size("wide")
     vmem = pl.BlockSpec(memory_space=pltpu.VMEM)
-    out_shape = [jax.ShapeDtypeStruct((hoods * 8, ROWS, ECELLS), jnp.float32)]
-    operands = [live, start, cond]
-    if with_rows:
-        out_shape.append(jax.ShapeDtypeStruct((hoods * 8,) + rows.shape[1:], jnp.float32))
-        operands.append(rows)
+    hbm = pl.BlockSpec(memory_space=pl.ANY)
+    f32 = jnp.float32
     return pl.pallas_call(
-        functools.partial(filter_kernel, chunk, with_rows),
-        in_specs=[pl.BlockSpec(memory_space=pltpu.SMEM)] + [vmem] * len(operands),
-        out_specs=[vmem] * len(out_shape),
+        exchange_kernel,
+        in_specs=[pl.BlockSpec(memory_space=pltpu.SMEM)] + [vmem] * 5,
+        out_specs=[hbm] * 3,
+        out_shape=[
+            jax.ShapeDtypeStruct((3, pieces, ROWS, ECELLS), f32),
+            jax.ShapeDtypeStruct((pieces, 16, LANES), f32),
+            jax.ShapeDtypeStruct((wides,) + ids.shape, jnp.int32),
+        ],
         scratch_shapes=[
-            pltpu.VMEM((5, CELLS, LANES), jnp.float32),
-            pltpu.VMEM((FIELD, LANES), jnp.float32),
-            pltpu.VMEM((FIELD, LANES), jnp.float32),
-            pltpu.VMEM((PLANE, LANES), jnp.float32),
+            pltpu.VMEM((5, CELLS, LANES), f32),
+            pltpu.VMEM((FIELD, LANES), f32),
+            pltpu.VMEM((FIELD, LANES), f32),
+            pltpu.VMEM((PLANE, LANES), f32),
+            pltpu.VMEM((pieces, ROWS, ECELLS), f32),
+            pltpu.VMEM((3, pieces, ROWS, ECELLS), f32),
+            pltpu.VMEM((hoods, 48, LANES), f32),
+            pltpu.VMEM((pieces, 16, LANES), f32),
+            pltpu.SemaphoreType.DMA((6,)),
+            pltpu.SemaphoreType.DMA((6,)),
+            pltpu.SemaphoreType.DMA((6,)),
         ],
-        out_shape=out_shape,
-        compiler_params=pltpu.CompilerParams(vmem_limit_bytes=48 * 2**20),
-        cost_estimate=pl.CostEstimate(
-            flops=hoods * ROWS * CELLS * 120, bytes_accessed=6 * 2**20, transcendentals=0
-        ),
-        name="filter",
-    )(dest, *operands)
+        compiler_params=pltpu.CompilerParams(has_side_effects=True, vmem_limit_bytes=48 * 2**20),
+        name="exchange",
+    )(order, live, start, cond, coarse, ids)
 
 
 def split(wide_value):
@@ -223,12 +321,12 @@
 
 
 def element_kernel(where, weight, *rest):
-    pieces, rows = rest[:24], rest[24:32]
-    out, back, high, low, vec_high, vec_low = rest[32:]
+    pieces, rows = rest[:8], rest[8:16]
+    out, back, high, low, vec_high, vec_low = rest[16:]
     element = pl.program_id(0)
     root = jnp.sqrt(weight[0]) * (1.0 / ECELLS) ** 0.5
     for o in range(8):
-        parts = [pieces[o * 3 + ch][0, g] for g in range(4) for ch in range(3)]
+        parts = [pieces[o][ch, 0, g] for g in range(4) for ch in range(3)]
         whole = jnp.concatenate(parts, axis=0) * root
         high[pl.ds(o * 96, 96)], low[pl.ds(o * 96, 96)] = split(whole)
         packed = rows[o][0]
@@ -259,10 +357,10 @@
 
 def elements(where, weight, got, rows):
     count = weight.shape[0]
-    sources = got[0].shape[0]
+    sources = got.shape[1]
 
     def piece(o):
-        return pl.BlockSpec((1, 4, ROWS, ECELLS), lambda e, where: (where[e * 8 + o], 0, 0, 0))
+        return pl.BlockSpec((3, 1, 4, ROWS, ECELLS), lambda e, where: (0, where[e * 8 + o], 0, 0, 0))
 
     def vecs(o):
         return pl.BlockSpec((1, 4, 16, LANES), lambda e, where: (where[e * 8 + o], 0, 0, 0))
@@ -273,7 +371,7 @@
             num_scalar_prefetch=1,
             grid=(count,),
             in_specs=[pl.BlockSpec((1, 1, ECELLS), lambda e, where: (e, 0, 0))]
-            + [piece(o) for o in range(8) for _ in range(3)]
+            + [piece(o) for o in range(8)]
             + [vecs(o) for o in range(8)],
             out_specs=[
                 pl.BlockSpec((1, 768, 768), lambda e, where: (e, 0, 0)),
@@ -292,65 +390,101 @@
         ],
         compiler_params=pltpu.CompilerParams(vmem_limit_bytes=48 * 2**20),
         name="elements",
-    )(where, weight, *[got[ch] for _ in range(8) for ch in range(3)], *[rows] * 8)
-
-
-def sum_kernel(dest, back, out):
-    hoods = out.shape[0]
-    for n in range(hoods):
-        total = back[dest[n * 8]]
+    )(where, weight, *[got] * 8, *[rows] * 8)
+
+
+def return_kernel(dest, back, out, returned, sums, send_sem, recv_sem, own_sem):
+    wide, eight = lax.axis_index("wide"), lax.axis_index("eight")
+    groups, wides = lax.axis_size("eight"), lax.axis_size("wide")
+    devices = groups * wides
+    me = wide * groups + eight
+    mine = out.shape[1]
+
+    def send(k, carry):
+        to_wide, to_eight = partner(k, wide, eight)
+        pltpu.make_async_remote_copy(
+            src_ref=back.at[to_wide, to_eight], dst_ref=returned.at[me], send_sem=send_sem.at[0],
+            recv_sem=recv_sem.at[0], device_id=(to_wide, to_eight), device_id_type=MESH,
+        ).start()
+        return carry
+
+    lax.fori_loop(1, devices, send, 0)
+    kept = pltpu.make_async_copy(back.at[wide, eight], returned.at[me], own_sem.at[0])
+    kept.start()
+    kept.wait()
+    others = returned.at[pl.ds(0, devices - 1)]
+    all_of(others)(recv_sem.at[0]).wait()
+    for n in range(mine * groups):
+        total = returned[dest[n * 8]]
         for o in range(1, 8):
-            total += back[dest[n * 8 + o]]
-        out[n] = total
-
-
-def summed(dest, back):
+            total += returned[dest[n * 8 + o]]
+        sums[n] = total
+    for k in range(1, groups):
+        to = (eight + k) % groups
+        pltpu.make_async_remote_copy(
+            src_ref=sums.at[pl.ds(to * mine, mine)], dst_ref=out.at[eight], send_sem=send_sem.at[1],
+            recv_sem=recv_sem.at[1], device_id=(wide, to), device_id_type=MESH,
+        ).start()
+    kept = pltpu.make_async_copy(sums.at[pl.ds(eight * mine, mine)], out.at[eight], own_sem.at[1])
+    kept.start()
+    kept.wait()
+    three = out.at[pl.ds(0, groups - 1)]
+    all_of(three)(recv_sem.at[1]).wait()
+    all_of(three)(send_sem.at[1]).wait()
+    all_of(others)(send_sem.at[0]).wait()
+
+
+def returned_sums(dest, back):
     hoods = dest.shape[0] // 8
+    groups = lax.axis_size("eight")
+    devices = back.shape[0] * groups
+    vmem = pl.BlockSpec(memory_space=pltpu.VMEM)
     return pl.pallas_call(
-        sum_kernel,
-        in_specs=[pl.BlockSpec(memory_space=pltpu.SMEM), pl.BlockSpec(memory_space=pltpu.VMEM)],
-        out_specs=pl.BlockSpec(memory_space=pltpu.VMEM),
-        out_shape=jax.ShapeDtypeStruct((hoods,) + back.shape[1:], jnp.float32),
-        name="sums",
+        return_kernel,
+        in_specs=[pl.BlockSpec(memory_space=pltpu.SMEM), vmem],
+        out_specs=vmem,
+        out_shape=jax.ShapeDtypeStruct((groups, hoods // groups, 16, LANES), jnp.float32),
+        scratch_shapes=[
+            pltpu.VMEM((devices, 16, LANES), jnp.float32),
+            pltpu.VMEM((hoods, 16, LANES), jnp.float32),
+            pltpu.SemaphoreType.DMA((2,)),
+            pltpu.SemaphoreType.DMA((2,)),
+            pltpu.SemaphoreType.DMA((2,)),
+        ],
+        compiler_params=pltpu.CompilerParams(has_side_effects=True, vmem_limit_bytes=16 * 2**20),
+        name="returns",
     )(dest, back)
 
 
 def body(start_vectors, conductance, counts, element_of, capacity, coarse_in):
-    me = lax.axis_index("wide") * 4 + lax.axis_index("eight")
-    group = lax.axis_index("eight")
+    eight = lax.axis_index("eight")
+    me = lax.axis_index("wide") * lax.axis_size("eight") + eight
     hoods = start_vectors.shape[0]
     count = capacity.shape[0]
     dest = (element_of // count).reshape(-1)
-    everyone = lax.all_gather(element_of, "wide")
-    names = me * count + jnp.arange(count, dtype=jnp.int32)
-    hits = everyone[None] == names[:, None, None, None]
-    indices = jnp.arange(everyone.shape[0], dtype=jnp.int32)[None, :, None, None]
-    where = jnp.sum(jnp.where(hits, indices, 0), axis=(1, 2)).reshape(-1)
-
-    packed = jnp.concatenate([coarse_in[:, :48], coarse_in[:, 48:]], axis=2)
-    packed = lax.all_gather(packed, "eight", tiled=True)
-    rows = lax.dynamic_slice_in_dim(packed, jnp.minimum(group, 2) * 16, 16, axis=1)
-
-    slots = group * 24 + jnp.arange(24, dtype=jnp.int32).reshape(3, 1, ROWS)
+    pieces = dest.shape[0]
+    names = jnp.arange(pieces, dtype=jnp.int32)
+    places = (element_of % count * 8 + jnp.arange(8, dtype=jnp.int32)[None, :]).reshape(-1)
+    both = names * 1024 + places
+    both = jnp.sum(jnp.where(dest[None, :] == names[:, None], both[None, :], 0), axis=1)
+    order, ids = both // 1024, both % 1024
+    slots = eight * 24 + jnp.arange(24, dtype=jnp.int32).reshape(3, 1, ROWS)
     live = (slots < counts[None, :, None]).astype(jnp.float32).reshape(3, LANES)
-    send = functools.partial(lax.all_to_all, axis_name=BOTH, split_axis=0, concat_axis=0, tiled=True)
-    got = []
-    rows_out = None
-    for chunk in range(3):
-        out = filtered(
-            chunk, dest, live, start_vectors, conductance, rows if chunk == 2 else None
-        )
-        if chunk == 2:
-            rows_out = out[1]
-        got.append(send(out[0]).reshape(-1, 4, ROWS, ECELLS))
-    got_rows = send(rows_out).reshape(-1, 4, 16, LANES)
-
-    weight = capacity.reshape(count, 1, ECELLS)
-    galerkin, back = elements(where, weight, got, got_rows)
-    back = send(back.reshape(-1, 16, LANES))
-    sums = summed(dest, back)
-    mine = lax.all_to_all(sums, "eight", split_axis=0, concat_axis=0, tiled=True)
-    mine = mine.reshape(4, hoods // 4, 16, LANES)[:3].transpose(1, 0, 2, 3).reshape(hoods // 4, 48, LANES)
+    got, got_rows, table = exchanged(
+        order, live, start_vectors, conductance, coarse_in, jnp.broadcast_to(ids[None], (8, pieces))
+    )
+    wides = table.shape[0]
+    came = lax.dynamic_slice_in_dim(table[:, 0], me, 1, axis=1)
+    spots = jnp.arange(count * 8, dtype=jnp.int32)[None]
+    sources = jnp.arange(wides, dtype=jnp.int32)[:, None]
+    where = jnp.sum(jnp.where(came == spots, sources, 0), axis=0)
+    galerkin, back = elements(
+        where,
+        capacity.reshape(count, 1, ECELLS),
+        got.reshape(3, wides, 4, ROWS, ECELLS),
+        got_rows.reshape(wides, 4, 16, LANES),
+    )
+    mine = returned_sums(dest, back)[:3].transpose(1, 0, 2, 3).reshape(hoods // 4, 48, LANES)
     coarse_out = jnp.concatenate([mine[:, :, :64], mine[:, :, 64:]], axis=1)
     return (galerkin, coarse_out)
 

time: 241 us -> 161 us (0.67)
  blocking collectives: 126 us -> 0 us
  Pallas kernels: 65.2 us -> 152 us
  starting transfers between devices: 26.9 us -> 0 us
  waiting for transfers between devices: 10.7 us -> 0 us
  local copies, waits for them, and re-layouts: 9.83 us -> 7.4 us
    pallas_call x4 -> x2, Pallas kernels: 52.1 us -> 139 us  [the longest x1 109 us: exchanged(): pl.pallas_call(exchange_kernel, in_specs=[pl.BlockSpec(memory_space=pltpu...]
    all_to_all x3 -> x0, blocking collectives: 69.6 us -> none  [the longest x1 34.7 us: body(): got.append(send(out[0]).reshape(-1, 4, ROWS, ECELLS))]
    all_gather x2 -> x0, blocking collectives: 56 us -> none  [the longest x1 42.9 us: body(): everyone = lax.all_gather(element_of, 'wide')]
    all_to_all x3 -> x0, starting transfers between devices: 26.9 us -> none  [the longest x2 16.2 us: body(): got.append(send(out[0]).reshape(-1, 4, ROWS, ECELLS))]
    all_to_all x3 -> x0, waiting for transfers between devices: 10.7 us -> none  [the longest x2 10.7 us: body(): got.append(send(out[0]).reshape(-1, 4, ROWS, ECELLS))]
    unnamed x19 -> x6, local copies, waits for them, and re-layouts: 7.38 us -> 4.62 us
  transfers between devices with their start and end apart: 3 -> 0, of which waited for: 1 -> 0; matrix products, arithmetic and copies ran while one was open for 0% -> 0% of each run, Pallas kernels for 13% -> 0%
where the time goes in v2:
time: 161 us
  Pallas kernels  152 us (94%)
  local copies, waits for them, and re-layouts  7.4 us (5%)
    pallas_call x1, Pallas kernels, exchanged(): pl.pallas_call(exchange_kernel, in_specs=[pl.BlockSpec(memory_space=pltpu...  109 us
    pallas_call x1, Pallas kernels, returned_sums(): pl.pallas_call(return_kernel, in_specs=[pl.BlockSpec(memory_space=pltpu.S...  29.5 us
    pallas_call x1, Pallas kernels, elements(): pl.pallas_call(element_kernel, grid_spec=pltpu.PrefetchScalarGridSpec(num...  13.4 us
    unnamed x6, local copies, waits for them, and re-layouts  4.62 us

profile of v2, /device:TPU:0, one launch (start us, length us, event | category | flops | bytes accessed | tf_op | source)
XLA Modules:
  0.0 161.1 jit_solution(1040060134835244510)
XLA Ops:
  0.6 0.7 lt.38
  1.4 0.1 lt.39
  1.5 0.7 reshape.75.weight
  2.2 0.7 add_select_fusion.1
  2.9 0.1 copy.16
  2.9 0.1 eq.34.dest
  3.0 0.1 copy.17
  3.1 0.1 reshape.71
  3.2 0.1 select_reduce_fusion
  3.4 0.1 lt.37
  3.5 1.0 copy.18.coarse
  4.5 0.0 copy-start
  4.5 1.9 %copy-done = bf16[16,24,4096]{2,1,0:T(8,128)(2,1)S(1)} copy-done((bf16[16,24,4096]{2,1,0:T(8,128)(2,1)S(1)}, bf16[16,24,4096]{2,1,0:T(8,128)(2,1)}, u32[]{:S(2)}) %copy-start) | copy-done | bytes 3145752
  6.4 0.0 copy-start.1
  6.4 0.9 copy-done.1
  7.3 109.0 %exchange.1 = (f32[3,128,8,512]{3,2,1,0:T(8,128)}, f32[128,16,128]{2,1,0:T(8,128)S(1)}, s32[32,8,128]{2,1,0:T(8,128)S(1)}) custom-call(s32[128]{0:T(128)S(1)} %get-tuple-element.21.order, f32[3,128]{1,0:T(4,128)S(1)} %compare_convert_fusion.live, bf16[16,24,4096]{2,1,0:T(8,128)(2,1)S(1)} %copy-done, f32[16,4096]{1,0:T(8,128)S(1)} %copy-done.1, ...), custom_call_target="tpu_custom_call" | custom-call | tf_op jit(solution)/shard_map/exchange/pallas_call | solution.py:283
  116.4 0.7 dynamic-slice_reduce_fusion
  117.1 0.1 select_reduce_fusion.1.where
  117.2 13.4 %elements.1 = (f32[4,768,768]{2,1,0:T(8,128)}, f32[32,4,16,128]{3,2,1,0:T(8,128)S(1)}) custom-call(s32[32]{0:T(128)S(1)} %select_reduce_fusion.1.where, f32[4,1,512]{2,1,0:T(1,128)S(1)} %reshape.75.weight, f32[3,32,4,8,512]{4,3,2,1,0:T(8,128)} %bitcast.13, f32[3,32,4,8,512]{4,3,2,1,0:T(8,128)} %bitcast.14, f32[3,32,4,8,512]{4,3,2,1,0:T(8,128)} %bitcast.15, ...), custom_call_target="tpu_custom_call" | custom-call | tf_op jit(solution)/shard_map/elements/pallas_call | solution.py:368
  130.7 29.5 %returns.1 = f32[4,4,16,128]{3,2,1,0:T(8,128)S(1)} custom-call(s32[128]{0:T(128)S(1)} %eq.34.dest, f32[32,4,16,128]{3,2,1,0:T(8,128)S(1)} %get-tuple-element.11.back), custom_call_target="tpu_custom_call" | custom-call | tf_op jit(solution)/shard_map/returns/pallas_call | solution.py:442
  160.2 0.1 fusion.4
  160.3 0.8 copy.20
  (10 shorter events, 0.1 us)
Async XLA Ops:
  4.5 1.9 %copy-start = (bf16[16,24,4096]{2,1,0:T(8,128)(2,1)S(1)}, bf16[16,24,4096]{2,1,0:T(8,128)(2,1)}, u32[]{:S(2)}) copy-start(bf16[16,24,4096]{2,1,0:T(8,128)(2,1)} %start.1) | copy-start | bytes 9437188
  6.4 0.9 copy-start.1

commit v3 on v2

--- a/solution.py
+++ b/solution.py
@@ -123,7 +123,7 @@
     return lax.fori_loop(0, SIDE, one, jnp.zeros((SIDE, LANES), jnp.float32))
 
 
-def filtered_chunk(chunk, start, coef, even, odd, flux):
+def filtered_chunk(chunk, start, coef, even, odd, flux, meanwhile=None):
     hoods, width = start.shape[:2]
     clear_ends(even)
     clear_ends(odd)
@@ -136,6 +136,8 @@
 
     lax.fori_loop(0, SIDE, bring, 0)
     sweep(coef, even, odd, flux, first=True)
+    if meanwhile is not None:
+        meanwhile()
 
     def two(step, carry):
         sweep(coef, odd, even, flux)
@@ -164,11 +166,24 @@
 
 
 def partner(k, wide, eight):
-    z, x, core = wide // 8, wide // 2 % 4, wide % 2
-    z = (z + k // 16 + 2 * (k // 4) + 3 * k) % 4
-    x = (x + k // 4 + k) % 4
-    core = (core + k // 64 + k) % 2
-    return (z * 4 + x) * 2 + core, (eight + k) % 4
+    z, x, core, four = wide >> 3, wide >> 1, wide, k >> 2
+    z = (z + (k >> 4) + 2 * four + 3 * k) & 3
+    x = (x + four + k) & 3
+    core = (core + (k >> 6) + k) & 1
+    return (z * 4 + x) * 2 + core, (eight + k) & 3
+
+
+def greet(wide, eight):
+    barrier = pltpu.get_barrier_semaphore()
+    devices = lax.axis_size("wide") * lax.axis_size("eight")
+
+    def one(k, carry):
+        to = partner(k, wide, eight)
+        pl.semaphore_signal(barrier, inc=1, device_id=to, device_id_type=MESH)
+        return carry
+
+    lax.fori_loop(1, devices, one, 0)
+    return lambda: pl.semaphore_wait(barrier, devices - 1)
 
 
 def all_of(ref):
@@ -188,9 +203,12 @@
     hoods = start.shape[0]
     mine = coarse.shape[0]
 
+    all_here = greet(wide, eight)
+    link_weights(cond, coef, even)
     for n in range(mine):
         packed = jnp.concatenate([coarse[n, :48], coarse[n, 48:]], axis=1)
         coarse_rows[pl.ds(eight * mine + n, 1)] = packed[None]
+    all_here()
     own_rows = coarse_rows.at[pl.ds(eight * mine, mine)]
     for k in range(1, groups):
         pltpu.make_async_remote_copy(
@@ -209,11 +227,7 @@
     own_ids = pltpu.make_async_copy(ids, table.at[wide], own_sem.at[4])
     own_ids.start()
 
-    link_weights(cond, coef, even)
-
     three = coarse_rows.at[pl.ds(0, mine * (groups - 1))]
-    all_of(three)(recv_sem.at[3]).wait()
-
     first = jnp.minimum(eight, 2) * 16
 
     def take_rows(to):
@@ -229,13 +243,19 @@
         ).start()
         return carry
 
-    lax.fori_loop(1, devices, send_rows, 0)
-    take_rows(me)
     kept_rows = pltpu.make_async_copy(outgoing_rows.at[me], got_rows.at[me], own_sem.at[5])
-    kept_rows.start()
+
+    def send_all_rows():
+        all_of(three)(recv_sem.at[3]).wait()
+        lax.fori_loop(1, devices, send_rows, 0)
+        take_rows(me)
+        kept_rows.start()
+
     kept = []
     for chunk in range(3):
-        mean = filtered_chunk(chunk, start, coef, even, odd, flux)
+        mean = filtered_chunk(
+            chunk, start, coef, even, odd, flux, send_all_rows if chunk == 0 else None
+        )
         scale = jnp.broadcast_to(lax.rsqrt(mean + 1e-05) * live[chunk : chunk + 1], (8, LANES))
         for octant in range(8):
             turned = octant_of(even, scale, octant)
@@ -302,7 +322,8 @@
             pltpu.SemaphoreType.DMA((6,)),
             pltpu.SemaphoreType.DMA((6,)),
         ],
-        compiler_params=pltpu.CompilerParams(has_side_effects=True, vmem_limit_bytes=48 * 2**20),
+        compiler_params=pltpu.CompilerParams(
+            collective_id=0, has_side_effects=True, vmem_limit_bytes=48 * 2**20),
         name="exchange",
     )(order, live, start, cond, coarse, ids)
 
@@ -320,85 +341,49 @@
     return dot(lh, rh) + (dot(lh, rl) + dot(ll, rh))
 
 
-def element_kernel(where, weight, *rest):
-    pieces, rows = rest[:8], rest[8:16]
-    out, back, high, low, vec_high, vec_low = rest[16:]
-    element = pl.program_id(0)
-    root = jnp.sqrt(weight[0]) * (1.0 / ECELLS) ** 0.5
-    for o in range(8):
-        parts = [pieces[o][ch, 0, g] for g in range(4) for ch in range(3)]
-        whole = jnp.concatenate(parts, axis=0) * root
-        high[pl.ds(o * 96, 96)], low[pl.ds(o * 96, 96)] = split(whole)
-        packed = rows[o][0]
-        packed = jnp.concatenate([packed[g] for g in range(3)], axis=0)
-        vec = jnp.concatenate([packed[:, :64], packed[:, 64:]], axis=0)
-        vec_high[pl.ds(o * 96, 96)], vec_low[pl.ds(o * 96, 96)] = split(vec)
-
-    def block(i):
-        return pl.ds(i * 256, 256)
-
-    for i in range(3):
-        for j in range(i, 3):
-            product = thrice(
-                (high[block(i)], low[block(i)]), (high[block(j)], low[block(j)]), ((1,), (1,))
-            )
-            out[0, block(i), block(j)] = product
-            if i != j:
-                out[0, block(j), block(i)] = product.T
-    vec = (vec_high[...], vec_low[...])
-    for i in range(8):
-        applied = thrice(split(out[0, pl.ds(i * 96, 96)]), vec, ((1,), (0,)))
-        packed = jnp.concatenate([applied[:48], applied[48:]], axis=1)
-        source = where[element * 8 + i]
-        for g in range(3):
-            back[source, g] = packed[g * 16 : (g + 1) * 16]
-        back[source, 3] = jnp.zeros((16, LANES), jnp.float32)
-
-
-def elements(where, weight, got, rows):
-    count = weight.shape[0]
-    sources = got.shape[1]
-
-    def piece(o):
-        return pl.BlockSpec((3, 1, 4, ROWS, ECELLS), lambda e, where: (0, where[e * 8 + o], 0, 0, 0))
-
-    def vecs(o):
-        return pl.BlockSpec((1, 4, 16, LANES), lambda e, where: (where[e * 8 + o], 0, 0, 0))
-
-    return pl.pallas_call(
-        element_kernel,
-        grid_spec=pltpu.PrefetchScalarGridSpec(
-            num_scalar_prefetch=1,
-            grid=(count,),
-            in_specs=[pl.BlockSpec((1, 1, ECELLS), lambda e, where: (e, 0, 0))]
-            + [piece(o) for o in range(8)]
-            + [vecs(o) for o in range(8)],
-            out_specs=[
-                pl.BlockSpec((1, 768, 768), lambda e, where: (e, 0, 0)),
-                pl.BlockSpec((sources, 4, 16, LANES), lambda e, where: (0, 0, 0, 0)),
-            ],
-            scratch_shapes=[
-                pltpu.VMEM((768, ECELLS), jnp.bfloat16),
-                pltpu.VMEM((768, ECELLS), jnp.bfloat16),
-                pltpu.VMEM((768, 64), jnp.bfloat16),
-                pltpu.VMEM((768, 64), jnp.bfloat16),
-            ],
-        ),
-        out_shape=[
-            jax.ShapeDtypeStruct((count, 768, 768), jnp.float32),
-            jax.ShapeDtypeStruct((sources, 4, 16, LANES), jnp.float32),
-        ],
-        compiler_params=pltpu.CompilerParams(vmem_limit_bytes=48 * 2**20),
-        name="elements",
-    )(where, weight, *[got] * 8, *[rows] * 8)
-
-
-def return_kernel(dest, back, out, returned, sums, send_sem, recv_sem, own_sem):
+def finish_kernel(
+    where, places, dest, weight, pieces, rows,
+    galerkin, out,
+    high, low, applied, back, made, returned, sums, send_sem, recv_sem, own_sem, out_sem,
+):
     wide, eight = lax.axis_index("wide"), lax.axis_index("eight")
     groups, wides = lax.axis_size("eight"), lax.axis_size("wide")
     devices = groups * wides
     me = wide * groups + eight
     mine = out.shape[1]
+    count = weight.shape[0]
+    all_here = greet(wide, eight)
+
+    def apply(element, carry):
+        root = jnp.sqrt(weight[element]) * (1.0 / ECELLS) ** 0.5
+        vecs = []
+        for o in range(8):
+            source = where[element * 8 + o]
+            parts = [pieces[ch, source, g] for g in range(4) for ch in range(3)]
+            whole = jnp.concatenate(parts, axis=0) * root
+            high[element, pl.ds(o * 96, 96)], low[element, pl.ds(o * 96, 96)] = split(whole)
+            packed = jnp.concatenate([rows[source, g] for g in range(3)], axis=0)
+            vecs += [packed[:, :64], packed[:, 64:]]
+        vec = jnp.concatenate(vecs, axis=0).T
+        whole = (high[element], low[element])
+        seen = thrice(split(vec), whole, ((1,), (0,)))
+        product = thrice(whole, split(seen), ((1,), (1,)))
+        for o in range(8):
+            halves = [product[o * 96 + h * 48 : o * 96 + h * 48 + 48] for h in range(2)]
+            applied[element * 8 + o] = jnp.concatenate(halves, axis=1)
+        return carry
+
+    lax.fori_loop(0, count, apply, 0)
+
+    def place(source, carry):
+        packed = applied[places[source]]
+        for g in range(3):
+            back[source, g] = packed[g * 16 : g * 16 + 16]
+        back[source, 3] = jnp.zeros((16, LANES), jnp.float32)
+        return carry
+
+    lax.fori_loop(0, wides, place, 0)
+    all_here()
 
     def send(k, carry):
         to_wide, to_eight = partner(k, wide, eight)
@@ -411,16 +396,37 @@
     lax.fori_loop(1, devices, send, 0)
     kept = pltpu.make_async_copy(back.at[wide, eight], returned.at[me], own_sem.at[0])
     kept.start()
+
+    def matrix(element, carry):
+        def block(i):
+            return element, pl.ds(i * 256, 256)
+
+        for i in range(3):
+            for j in range(i, 3):
+                product = thrice(
+                    (high[block(i)], low[block(i)]), (high[block(j)], low[block(j)]), ((1,), (1,))
+                )
+                made[element, pl.ds(i * 256, 256), pl.ds(j * 256, 256)] = product
+                if i != j:
+                    made[element, pl.ds(j * 256, 256), pl.ds(i * 256, 256)] = product.T
+        pltpu.make_async_copy(made.at[element], galerkin.at[element], out_sem.at[element]).start()
+        return carry
+
+    lax.fori_loop(0, count, matrix, 0)
     kept.wait()
     others = returned.at[pl.ds(0, devices - 1)]
     all_of(others)(recv_sem.at[0]).wait()
-    for n in range(mine * groups):
+
+    def total_of(n, carry):
         total = returned[dest[n * 8]]
         for o in range(1, 8):
             total += returned[dest[n * 8 + o]]
         sums[n] = total
+        return carry
+
+    lax.fori_loop(0, mine * groups, total_of, 0)
     for k in range(1, groups):
-        to = (eight + k) % groups
+        to = (eight + k) & 3
         pltpu.make_async_remote_copy(
             src_ref=sums.at[pl.ds(to * mine, mine)], dst_ref=out.at[eight], send_sem=send_sem.at[1],
             recv_sem=recv_sem.at[1], device_id=(wide, to), device_id_type=MESH,
@@ -432,28 +438,44 @@
     all_of(three)(recv_sem.at[1]).wait()
     all_of(three)(send_sem.at[1]).wait()
     all_of(others)(send_sem.at[0]).wait()
-
-
-def returned_sums(dest, back):
+    for element in range(count):
+        pltpu.make_async_copy(made.at[element], galerkin.at[element], out_sem.at[element]).wait()
+
+
+def finished(where, places, dest, weight, got, rows):
     hoods = dest.shape[0] // 8
+    count = weight.shape[0]
     groups = lax.axis_size("eight")
-    devices = back.shape[0] * groups
-    vmem = pl.BlockSpec(memory_space=pltpu.VMEM)
+    wides = got.shape[1]
+    devices = wides * groups
+    smem, vmem = (pl.BlockSpec(memory_space=m) for m in (pltpu.SMEM, pltpu.VMEM))
+    f32 = jnp.float32
     return pl.pallas_call(
-        return_kernel,
-        in_specs=[pl.BlockSpec(memory_space=pltpu.SMEM), vmem],
-        out_specs=vmem,
-        out_shape=jax.ShapeDtypeStruct((groups, hoods // groups, 16, LANES), jnp.float32),
+        finish_kernel,
+        in_specs=[smem] * 3 + [vmem] * 3,
+        out_specs=[pl.BlockSpec(memory_space=pl.ANY), vmem],
+        out_shape=[
+            jax.ShapeDtypeStruct((count, 768, 768), f32),
+            jax.ShapeDtypeStruct((groups, hoods // groups, 16, LANES), f32),
+        ],
         scratch_shapes=[
-            pltpu.VMEM((devices, 16, LANES), jnp.float32),
-            pltpu.VMEM((hoods, 16, LANES), jnp.float32),
+            pltpu.VMEM((count, 768, ECELLS), jnp.bfloat16),
+            pltpu.VMEM((count, 768, ECELLS), jnp.bfloat16),
+            pltpu.VMEM((count * 8, 48, LANES), f32),
+            pltpu.VMEM((wides, groups, 16, LANES), f32),
+            pltpu.VMEM((count, 768, 768), f32),
+            pltpu.VMEM((devices, 16, LANES), f32),
+            pltpu.VMEM((hoods, 16, LANES), f32),
             pltpu.SemaphoreType.DMA((2,)),
             pltpu.SemaphoreType.DMA((2,)),
             pltpu.SemaphoreType.DMA((2,)),
+            pltpu.SemaphoreType.DMA((count,)),
         ],
-        compiler_params=pltpu.CompilerParams(has_side_effects=True, vmem_limit_bytes=16 * 2**20),
-        name="returns",
-    )(dest, back)
+        compiler_params=pltpu.CompilerParams(
+            collective_id=1, has_side_effects=True, vmem_limit_bytes=40 * 2**20
+        ),
+        name="finish",
+    )(where, places, dest, weight, got, rows)
 
 
 def body(start_vectors, conductance, counts, element_of, capacity, coarse_in):
@@ -478,13 +500,15 @@
     spots = jnp.arange(count * 8, dtype=jnp.int32)[None]
     sources = jnp.arange(wides, dtype=jnp.int32)[:, None]
     where = jnp.sum(jnp.where(came == spots, sources, 0), axis=0)
-    galerkin, back = elements(
+    galerkin, mine = finished(
         where,
+        came[:, 0],
+        dest,
         capacity.reshape(count, 1, ECELLS),
         got.reshape(3, wides, 4, ROWS, ECELLS),
         got_rows.reshape(wides, 4, 16, LANES),
     )
-    mine = returned_sums(dest, back)[:3].transpose(1, 0, 2, 3).reshape(hoods // 4, 48, LANES)
+    mine = mine[:3].transpose(1, 0, 2, 3).reshape(hoods // 4, 48, LANES)
     coarse_out = jnp.concatenate([mine[:, :, :64], mine[:, :, 64:]], axis=1)
     return (galerkin, coarse_out)
 

time: 161 us -> 151 us (0.938)
  Pallas kernels: 152 us -> 131 us
  local copies, waits for them, and re-layouts: 7.4 us -> 18.2 us
    pallas_call x2 -> x1, Pallas kernels: 43 us -> 30.8 us  [finished(): pl.pallas_call(finish_kernel, in_specs=[smem] * 3 + [vmem] * 3, out_specs...]
    unnamed x6 -> x9, local copies, waits for them, and re-layouts: 4.62 us -> 15.4 us
    pallas_call x1, Pallas kernels: 109 us -> 100 us  [exchanged(): pl.pallas_call(exchange_kernel, in_specs=[pl.BlockSpec(memory_space=pltpu...]
where the time goes in v3:
time: 151 us
  Pallas kernels  131 us (87%)
  local copies, waits for them, and re-layouts  18.2 us (12%)
    pallas_call x1, Pallas kernels, exchanged(): pl.pallas_call(exchange_kernel, in_specs=[pl.BlockSpec(memory_space=pltpu...  100 us
    pallas_call x1, Pallas kernels, finished(): pl.pallas_call(finish_kernel, in_specs=[smem] * 3 + [vmem] * 3, out_specs...  30.8 us
    unnamed x9, local copies, waits for them, and re-layouts  15.4 us

profile of v3, /device:TPU:0, one launch (start us, length us, event | category | flops | bytes accessed | tf_op | source)
XLA Modules:
  0.0 151.1 jit_solution(558762548995806424)
XLA Ops:
  0.6 0.7 lt.38
  1.4 0.1 lt.39
  1.5 0.7 reshape.76.weight
  2.2 0.7 add_select_fusion.1
  2.9 0.1 copy.16
  2.9 0.1 eq.34.dest
  3.0 0.1 copy.17
  3.1 0.1 reshape.72
  3.2 0.1 select_reduce_fusion
  3.4 0.1 lt.37
  3.5 1.0 copy.18.coarse
  4.5 0.0 copy-start.1
  4.5 1.9 %copy-done.1 = bf16[16,24,4096]{2,1,0:T(8,128)(2,1)S(1)} copy-done((bf16[16,24,4096]{2,1,0:T(8,128)(2,1)S(1)}, bf16[16,24,4096]{2,1,0:T(8,128)(2,1)}, u32[]{:S(2)}) %copy-start.1) | copy-done | bytes 3145752
  6.4 0.0 copy-start.2
  6.4 0.9 copy-done.2
  7.3 100.3 %exchange.1 = (f32[3,128,8,512]{3,2,1,0:T(8,128)}, f32[128,16,128]{2,1,0:T(8,128)S(1)}, s32[32,8,128]{2,1,0:T(8,128)S(1)}) custom-call(s32[128]{0:T(128)S(1)} %get-tuple-element.21.order, f32[3,128]{1,0:T(4,128)S(1)} %compare_convert_fusion.live, bf16[16,24,4096]{2,1,0:T(8,128)(2,1)S(1)} %copy-done.1, f32[16,4096]{1,0:T(8,128)S(1)} %copy-done.2, ...), custom_call_target="tpu_custom_call" | custom-call | tf_op jit(solution)/shard_map/exchange/pallas_call | solution.py:303
  107.7 0.7 dynamic-slice_reduce_fusion.places
  108.4 0.1 select_reduce_fusion.1.where
  108.5 0.0 copy-start
  108.5 2.8 %copy-done = f32[3,128,8,512]{3,2,1,0:T(8,128)S(1)} copy-done((f32[3,128,8,512]{3,2,1,0:T(8,128)S(1)}, f32[3,128,8,512]{3,2,1,0:T(8,128)}, u32[]{:S(2)}) %copy-start) | copy-done | bytes 6291480
  111.3 30.8 %finish.1 = (f32[4,768,768]{2,1,0:T(8,128)}, f32[4,4,16,128]{3,2,1,0:T(8,128)S(1)}) custom-call(s32[32]{0:T(128)S(1)} %select_reduce_fusion.1.where, s32[32]{0:T(128)S(1)} %dynamic-slice_reduce_fusion.places, s32[128]{0:T(128)S(1)} %eq.34.dest, f32[4,1,512]{2,1,0:T(1,128)S(1)} %reshape.76.weight, f32[3,32,4,8,512]{4,3,2,1,0:T(8,128)S(1)} %bitcast.5, ...), custom_call_target="tpu_custom_call" | custom-call | tf_op jit(solution)/shard_map/finish/pallas_call | solution.py:453
  142.1 0.1 fusion.4
  142.3 0.8 copy.20
  143.0 8.0 %copy.22 = f32[4,768,768]{2,1,0:T(8,128)} copy(f32[4,768,768]{2,1,0:T(8,128)} %get-tuple-element.24) | data formatting | bytes 18874368
  (10 shorter events, 0.1 us)
Async XLA Ops:
  4.5 1.9 %copy-start.1 = (bf16[16,24,4096]{2,1,0:T(8,128)(2,1)S(1)}, bf16[16,24,4096]{2,1,0:T(8,128)(2,1)}, u32[]{:S(2)}) copy-start(bf16[16,24,4096]{2,1,0:T(8,128)(2,1)} %start.1) | copy-start | bytes 9437188
  6.4 0.9 copy-start.2
  108.5 2.8 %copy-start = (f32[3,128,8,512]{3,2,1,0:T(8,128)S(1)}, f32[3,128,8,512]{3,2,1,0:T(8,128)}, u32[]{:S(2)}) copy-start(f32[3,128,8,512]{3,2,1,0:T(8,128)} %get-tuple-element.8) | copy-start | bytes 18874372

commit v4 on v3

--- a/solution.py
+++ b/solution.py
@@ -206,7 +206,8 @@
     all_here = greet(wide, eight)
     link_weights(cond, coef, even)
     for n in range(mine):
-        packed = jnp.concatenate([coarse[n, :48], coarse[n, 48:]], axis=1)
+        turned = coarse[n].T
+        packed = jnp.concatenate([turned[:48], turned[48:]], axis=1)
         coarse_rows[pl.ds(eight * mine + n, 1)] = packed[None]
     all_here()
     own_rows = coarse_rows.at[pl.ds(eight * mine, mine)]
@@ -323,7 +324,7 @@
             pltpu.SemaphoreType.DMA((6,)),
         ],
         compiler_params=pltpu.CompilerParams(
-            collective_id=0, has_side_effects=True, vmem_limit_bytes=48 * 2**20),
+            collective_id=0, has_side_effects=True, vmem_limit_bytes=36 * 2**20),
         name="exchange",
     )(order, live, start, cond, coarse, ids)
 
@@ -355,7 +356,7 @@
     all_here = greet(wide, eight)
 
     def apply(element, carry):
-        root = jnp.sqrt(weight[element]) * (1.0 / ECELLS) ** 0.5
+        root = jnp.sqrt(weight[pl.ds(element, 1)])
         vecs = []
         for o in range(8):
             source = where[element * 8 + o]
@@ -367,7 +368,7 @@
         vec = jnp.concatenate(vecs, axis=0).T
         whole = (high[element], low[element])
         seen = thrice(split(vec), whole, ((1,), (0,)))
-        product = thrice(whole, split(seen), ((1,), (1,)))
+        product = thrice(whole, split(seen * (1.0 / ECELLS)), ((1,), (1,)))
         for o in range(8):
             halves = [product[o * 96 + h * 48 : o * 96 + h * 48 + 48] for h in range(2)]
             applied[element * 8 + o] = jnp.concatenate(halves, axis=1)
@@ -472,7 +473,7 @@
             pltpu.SemaphoreType.DMA((count,)),
         ],
         compiler_params=pltpu.CompilerParams(
-            collective_id=1, has_side_effects=True, vmem_limit_bytes=40 * 2**20
+            collective_id=1, has_side_effects=True, vmem_limit_bytes=28 * 2**20
         ),
         name="finish",
     )(where, places, dest, weight, got, rows)
@@ -493,7 +494,12 @@
     slots = eight * 24 + jnp.arange(24, dtype=jnp.int32).reshape(3, 1, ROWS)
     live = (slots < counts[None, :, None]).astype(jnp.float32).reshape(3, LANES)
     got, got_rows, table = exchanged(
-        order, live, start_vectors, conductance, coarse_in, jnp.broadcast_to(ids[None], (8, pieces))
+        order,
+        live,
+        start_vectors,
+        conductance,
+        coarse_in.transpose(0, 2, 1),
+        jnp.broadcast_to(ids[None], (8, pieces)),
     )
     wides = table.shape[0]
     came = lax.dynamic_slice_in_dim(table[:, 0], me, 1, axis=1)
@@ -504,10 +510,11 @@
         where,
         came[:, 0],
         dest,
-        capacity.reshape(count, 1, ECELLS),
+        capacity,
         got.reshape(3, wides, 4, ROWS, ECELLS),
         got_rows.reshape(wides, 4, 16, LANES),
     )
+    galerkin = galerkin * (1.0 / ECELLS)
     mine = mine[:3].transpose(1, 0, 2, 3).reshape(hoods // 4, 48, LANES)
     coarse_out = jnp.concatenate([mine[:, :, :64], mine[:, :, 64:]], axis=1)
     return (galerkin, coarse_out)

time: 151 us -> 145 us (0.960)
  local copies, waits for them, and re-layouts: 18.2 us -> 7.27 us
  other arithmetic: 0.95 us -> 5.59 us
    unnamed x9, local copies, waits for them, and re-layouts: 15.4 us -> 5.2 us
    mul x0 -> x1, other arithmetic: none -> 4.64 us  [body(): galerkin = galerkin * (1.0 / ECELLS)]
where the time goes in v4:
time: 145 us
  Pallas kernels  131 us (90%)
  local copies, waits for them, and re-layouts  7.27 us (5%)
  other arithmetic  5.59 us (4%)
    pallas_call x1, Pallas kernels, exchanged(): pl.pallas_call(exchange_kernel, in_specs=[pl.BlockSpec(memory_space=pltpu...  100 us
    pallas_call x1, Pallas kernels, finished(): pl.pallas_call(finish_kernel, in_specs=[smem] * 3 + [vmem] * 3, out_specs...  30.9 us
    unnamed x9, local copies, waits for them, and re-layouts  5.2 us
    mul x1, other arithmetic, body(): galerkin = galerkin * (1.0 / ECELLS)  4.64 us

profile of v4, /device:TPU:0, one launch (start us, length us, event | category | flops | bytes accessed | tf_op | source)
XLA Modules:
  0.0 144.7 jit_solution(18062787057078523095)
XLA Ops:
  0.6 0.7 lt.38
  1.4 0.1 lt.39
  1.5 0.7 add_select_fusion.1
  2.2 0.1 copy.14
  2.2 0.1 eq.34.dest
  2.3 0.1 copy.15
  2.4 0.1 reshape.69
  2.5 0.1 select_reduce_fusion
  2.7 0.1 lt.37
  2.8 0.0 copy-start
  2.8 1.9 %copy-done = bf16[16,24,4096]{2,1,0:T(8,128)(2,1)S(1)} copy-done((bf16[16,24,4096]{2,1,0:T(8,128)(2,1)S(1)}, bf16[16,24,4096]{2,1,0:T(8,128)(2,1)}, u32[]{:S(2)}) %copy-start) | copy-done | bytes 3145752
  4.7 0.0 copy-start.1
  4.7 0.9 copy-done.1
  5.6 0.0 copy-start.2
  5.6 0.9 copy-done.2
  6.5 100.2 %exchange.1 = (f32[3,128,8,512]{3,2,1,0:T(8,128)S(1)}, f32[128,16,128]{2,1,0:T(8,128)S(1)}, s32[32,8,128]{2,1,0:T(8,128)S(1)}) custom-call(s32[128]{0:T(128)S(1)} %get-tuple-element.21.order, f32[3,128]{1,0:T(4,128)S(1)} %compare_convert_fusion.live, bf16[16,24,4096]{2,1,0:T(8,128)(2,1)S(1)} %copy-done, f32[16,4096]{1,0:T(8,128)S(1)} %copy-done.1, ...), custom_call_target="tpu_custom_call" | custom-call | tf_op jit(solution)/shard_map/exchange/pallas_call | solution.py:304
  106.8 0.7 dynamic-slice_reduce_fusion.places
  107.5 0.1 select_reduce_fusion.1.where
  107.6 0.0 copy-start.3
  107.6 0.7 copy-done.3
  108.3 30.9 %finish.1 = (f32[4,768,768]{2,1,0:T(8,128)S(1)}, f32[4,4,16,128]{3,2,1,0:T(8,128)S(1)}) custom-call(s32[32]{0:T(128)S(1)} %select_reduce_fusion.1.where, s32[32]{0:T(128)S(1)} %dynamic-slice_reduce_fusion.places, s32[128]{0:T(128)S(1)} %eq.34.dest, f32[4,512]{1,0:T(4,128)S(1)} %copy-done.3, f32[3,32,4,8,512]{4,3,2,1,0:T(8,128)S(1)} %bitcast.6, ...), custom_call_target="tpu_custom_call" | custom-call | tf_op jit(solution)/shard_map/finish/pallas_call | solution.py:454
  139.1 4.6 %broadcast_multiply_fusion = f32[4,768,768]{2,1,0:T(8,128)} fusion(f32[4,768,768]{2,1,0:T(8,128)S(1)} %get-tuple-element.10), kind=kLoop, calls=%fused_computation | loop fusion | flops 2359296 | bytes 18874368 | tf_op jit(solution)/shard_map/mul | solution.py:517
  143.8 0.1 fusion.4
  143.9 0.8 copy.17
  (10 shorter events, 0.1 us)
Async XLA Ops:
  2.8 1.9 %copy-start = (bf16[16,24,4096]{2,1,0:T(8,128)(2,1)S(1)}, bf16[16,24,4096]{2,1,0:T(8,128)(2,1)}, u32[]{:S(2)}) copy-start(bf16[16,24,4096]{2,1,0:T(8,128)(2,1)} %start.1) | copy-start | bytes 9437188
  4.7 0.9 copy-start.1
  5.6 0.9 copy-start.2
  107.6 0.7 copy-start.3

commit v5 on v4

--- a/solution.py
+++ b/solution.py
@@ -13,6 +13,7 @@
 ECELLS = 512
 ROWS = 8
 LANES = 128
+SHARE = 12
 FRONT = 8
 FIELD = FRONT + CELLS + PLANE + 8
 GROUP = 4
@@ -29,7 +30,7 @@
     field[pl.ds(FRONT + CELLS, PLANE + 8)] = jnp.zeros((PLANE + 8, LANES), jnp.float32)
 
 
-def link_weights(cond, coef, field):
+def bring_conductance(cond, field):
     hoods = cond.shape[0]
     clear_ends(field)
 
@@ -40,6 +41,9 @@
         return carry
 
     lax.fori_loop(0, SIDE, bring, 0)
+
+
+def link_weights(coef, field):
     spot = lax.broadcasted_iota(jnp.int32, (SIDE, LANES), 0)
     ends = ((spot == 0) | (spot == SIDE - 1)).astype(jnp.float32)
 
@@ -191,9 +195,9 @@
 
 
 def exchange_kernel(
-    order, live, start, cond, coarse, ids,
+    order, counts, start, cond_hbm, coarse_hbm, ids,
     got, got_rows, table,
-    coef, even, odd, flux, pieces, outgoing, coarse_rows, outgoing_rows,
+    coef, even, odd, flux, pieces, outgoing, coarse_rows, outgoing_rows, cond, coarse,
     send_sem, recv_sem, own_sem,
 ):
     wide, eight = lax.axis_index("wide"), lax.axis_index("eight")
@@ -203,8 +207,20 @@
     hoods = start.shape[0]
     mine = coarse.shape[0]
 
+    bring_cond = pltpu.make_async_copy(cond_hbm, cond, own_sem.at[6])
+    bring_coarse = pltpu.make_async_copy(coarse_hbm, coarse, own_sem.at[7])
+    bring_cond.start()
+    bring_coarse.start()
     all_here = greet(wide, eight)
-    link_weights(cond, coef, even)
+    lane = lax.broadcasted_iota(jnp.int32, (8, LANES), 1)
+    limit = jnp.zeros((8, LANES), jnp.int32)
+    for n in range(hoods):
+        limit = jnp.where(lane // ROWS == n, counts[n], limit)
+    limit -= eight * 24 + lane % ROWS
+    bring_cond.wait()
+    bring_coarse.wait()
+    bring_conductance(cond, even)
+    link_weights(coef, even)
     for n in range(mine):
         turned = coarse[n].T
         packed = jnp.concatenate([turned[:48], turned[48:]], axis=1)
@@ -229,10 +245,10 @@
     own_ids.start()
 
     three = coarse_rows.at[pl.ds(0, mine * (groups - 1))]
-    first = jnp.minimum(eight, 2) * 16
+    first = eight * SHARE
 
     def take_rows(to):
-        outgoing_rows[pl.ds(to, 1)] = coarse_rows[pl.ds(order[to] // 8, 1), pl.ds(first, 16)]
+        outgoing_rows[pl.ds(to, 1)] = coarse_rows[pl.ds(order[to] // 8, 1), pl.ds(first, SHARE)]
 
     def send_rows(k, carry):
         to_wide, to_eight = partner(k, wide, eight)
@@ -257,7 +273,8 @@
         mean = filtered_chunk(
             chunk, start, coef, even, odd, flux, send_all_rows if chunk == 0 else None
         )
-        scale = jnp.broadcast_to(lax.rsqrt(mean + 1e-05) * live[chunk : chunk + 1], (8, LANES))
+        live = (limit > chunk * ROWS).astype(jnp.float32)
+        scale = jnp.broadcast_to(lax.rsqrt(mean + 1e-05), (8, LANES)) * live
         for octant in range(8):
             turned = octant_of(even, scale, octant)
             for n in range(hoods):
@@ -294,7 +311,7 @@
         all_of(others)(recv_sem.at[chunk]).wait()
 
 
-def exchanged(order, live, start, cond, coarse, ids):
+def exchanged(order, counts, start, cond, coarse, ids):
     hoods = start.shape[0]
     pieces = hoods * 8
     wides = lax.axis_size("wide")
@@ -303,11 +320,11 @@
     f32 = jnp.float32
     return pl.pallas_call(
         exchange_kernel,
-        in_specs=[pl.BlockSpec(memory_space=pltpu.SMEM)] + [vmem] * 5,
+        in_specs=[pl.BlockSpec(memory_space=pltpu.SMEM)] * 2 + [vmem, hbm, hbm, vmem],
         out_specs=[hbm] * 3,
         out_shape=[
             jax.ShapeDtypeStruct((3, pieces, ROWS, ECELLS), f32),
-            jax.ShapeDtypeStruct((pieces, 16, LANES), f32),
+            jax.ShapeDtypeStruct((pieces, SHARE, LANES), f32),
             jax.ShapeDtypeStruct((wides,) + ids.shape, jnp.int32),
         ],
         scratch_shapes=[
@@ -318,15 +335,17 @@
             pltpu.VMEM((pieces, ROWS, ECELLS), f32),
             pltpu.VMEM((3, pieces, ROWS, ECELLS), f32),
             pltpu.VMEM((hoods, 48, LANES), f32),
-            pltpu.VMEM((pieces, 16, LANES), f32),
+            pltpu.VMEM((pieces, SHARE, LANES), f32),
+            pltpu.VMEM(cond.shape, f32),
+            pltpu.VMEM(coarse.shape, f32),
             pltpu.SemaphoreType.DMA((6,)),
             pltpu.SemaphoreType.DMA((6,)),
-            pltpu.SemaphoreType.DMA((6,)),
+            pltpu.SemaphoreType.DMA((8,)),
         ],
         compiler_params=pltpu.CompilerParams(
             collective_id=0, has_side_effects=True, vmem_limit_bytes=36 * 2**20),
         name="exchange",
-    )(order, live, start, cond, coarse, ids)
+    )(order, counts, start, cond, coarse, ids)
 
 
 def split(wide_value):
@@ -363,7 +382,7 @@
             parts = [pieces[ch, source, g] for g in range(4) for ch in range(3)]
             whole = jnp.concatenate(parts, axis=0) * root
             high[element, pl.ds(o * 96, 96)], low[element, pl.ds(o * 96, 96)] = split(whole)
-            packed = jnp.concatenate([rows[source, g] for g in range(3)], axis=0)
+            packed = jnp.concatenate([rows[source, g] for g in range(4)], axis=0)
             vecs += [packed[:, :64], packed[:, 64:]]
         vec = jnp.concatenate(vecs, axis=0).T
         whole = (high[element], low[element])
@@ -378,9 +397,8 @@
 
     def place(source, carry):
         packed = applied[places[source]]
-        for g in range(3):
-            back[source, g] = packed[g * 16 : g * 16 + 16]
-        back[source, 3] = jnp.zeros((16, LANES), jnp.float32)
+        for g in range(4):
+            back[source, g] = packed[g * SHARE : (g + 1) * SHARE]
         return carry
 
     lax.fori_loop(0, wides, place, 0)
@@ -457,16 +475,16 @@
         out_specs=[pl.BlockSpec(memory_space=pl.ANY), vmem],
         out_shape=[
             jax.ShapeDtypeStruct((count, 768, 768), f32),
-            jax.ShapeDtypeStruct((groups, hoods // groups, 16, LANES), f32),
+            jax.ShapeDtypeStruct((groups, hoods // groups, SHARE, LANES), f32),
         ],
         scratch_shapes=[
             pltpu.VMEM((count, 768, ECELLS), jnp.bfloat16),
             pltpu.VMEM((count, 768, ECELLS), jnp.bfloat16),
             pltpu.VMEM((count * 8, 48, LANES), f32),
-            pltpu.VMEM((wides, groups, 16, LANES), f32),
+            pltpu.VMEM((wides, groups, SHARE, LANES), f32),
             pltpu.VMEM((count, 768, 768), f32),
-            pltpu.VMEM((devices, 16, LANES), f32),
-            pltpu.VMEM((hoods, 16, LANES), f32),
+            pltpu.VMEM((devices, SHARE, LANES), f32),
+            pltpu.VMEM((hoods, SHARE, LANES), f32),
             pltpu.SemaphoreType.DMA((2,)),
             pltpu.SemaphoreType.DMA((2,)),
             pltpu.SemaphoreType.DMA((2,)),
@@ -491,11 +509,9 @@
     both = names * 1024 + places
     both = jnp.sum(jnp.where(dest[None, :] == names[:, None], both[None, :], 0), axis=1)
     order, ids = both // 1024, both % 1024
-    slots = eight * 24 + jnp.arange(24, dtype=jnp.int32).reshape(3, 1, ROWS)
-    live = (slots < counts[None, :, None]).astype(jnp.float32).reshape(3, LANES)
     got, got_rows, table = exchanged(
         order,
-        live,
+        counts,
         start_vectors,
         conductance,
         coarse_in.transpose(0, 2, 1),
@@ -512,10 +528,10 @@
         dest,
         capacity,
         got.reshape(3, wides, 4, ROWS, ECELLS),
-        got_rows.reshape(wides, 4, 16, LANES),
+        got_rows.reshape(wides, 4, SHARE, LANES),
     )
     galerkin = galerkin * (1.0 / ECELLS)
-    mine = mine[:3].transpose(1, 0, 2, 3).reshape(hoods // 4, 48, LANES)
+    mine = mine.transpose(1, 0, 2, 3).reshape(hoods // 4, 48, LANES)
     coarse_out = jnp.concatenate([mine[:, :, :64], mine[:, :, 64:]], axis=1)
     return (galerkin, coarse_out)
 

time: 145 us -> 142 us (0.979)
  Pallas kernels: 131 us -> 128 us
    pallas_call x1, Pallas kernels: 30.9 us -> 27.8 us  [finished(): pl.pallas_call(finish_kernel, in_specs=[smem] * 3 + [vmem] * 3, out_specs...]
    unnamed x9 -> x11, local copies, waits for them, and re-layouts: 5.2 us -> 5.86 us
where the time goes in v5:
time: 142 us; the launch traced here: 141 us
  Pallas kernels  128 us (90%)
  local copies, waits for them, and re-layouts  7.08 us (5%)
  other arithmetic  5.61 us (4%)
    pallas_call x1, Pallas kernels, exchanged(): pl.pallas_call(exchange_kernel, in_specs=[pl.BlockSpec(memory_space=pltpu...  100 us
    pallas_call x1, Pallas kernels, finished(): pl.pallas_call(finish_kernel, in_specs=[smem] * 3 + [vmem] * 3, out_specs...  27.8 us
    unnamed x11, local copies, waits for them, and re-layouts  5.86 us
    mul x1, other arithmetic, body(): galerkin = galerkin * (1.0 / ECELLS)  4.64 us

profile of v5, /device:TPU:0, one launch (start us, length us, event | category | flops | bytes accessed | tf_op | source)
XLA Modules:
  0.0 141.3 jit_solution(13719678645221539746)
XLA Ops:
  0.6 0.7 add_select_fusion.1
  1.3 0.1 copy.14
  1.4 0.1 eq.34.dest
  1.5 0.1 copy.15
  1.6 0.1 reshape.43
  1.7 0.1 select_reduce_fusion
  1.8 0.0 copy-start
  1.8 1.9 %copy-done = bf16[16,24,4096]{2,1,0:T(8,128)(2,1)S(1)} copy-done((bf16[16,24,4096]{2,1,0:T(8,128)(2,1)S(1)}, bf16[16,24,4096]{2,1,0:T(8,128)(2,1)}, u32[]{:S(2)}) %copy-start) | copy-done | bytes 3145752
  3.7 0.0 copy-start.1
  3.7 0.9 copy-done.1
  4.7 0.0 copy-start.2
  4.7 0.9 copy-done.2
  5.6 0.0 copy-start.4
  5.6 0.7 copy-done.4
  6.2 100.1 %exchange.1 = (f32[3,128,8,512]{3,2,1,0:T(8,128)S(1)}, f32[128,12,128]{2,1,0:T(8,128)S(1)}, s32[32,8,128]{2,1,0:T(8,128)S(1)}) custom-call(s32[128]{0:T(128)S(1)} %get-tuple-element.21.order, s32[16]{0:T(128)S(1)} %copy-done.4, bf16[16,24,4096]{2,1,0:T(8,128)(2,1)S(1)} %copy-done, f32[16,4096]{1,0:T(8,128)S(1)} %copy-done.1, f32[4,64,96]{2,1,0:T(8,128)S(1)} %bitcast.7, ...), custom_call_target="tpu_custom_call" | custom-call | tf_op jit(solution)/shard_map/exchange/pallas_call | solution.py:321
  106.4 0.7 dynamic-slice_reduce_fusion.places
  107.1 0.1 select_reduce_fusion.1.where
  107.2 0.0 copy-start.3
  107.2 0.7 copy-done.3
  107.9 27.8 %finish.1 = (f32[4,768,768]{2,1,0:T(8,128)S(1)}, f32[4,4,12,128]{3,2,1,0:T(8,128)S(1)}) custom-call(s32[32]{0:T(128)S(1)} %select_reduce_fusion.1.where, s32[32]{0:T(128)S(1)} %dynamic-slice_reduce_fusion.places, s32[128]{0:T(128)S(1)} %eq.34.dest, f32[4,512]{1,0:T(4,128)S(1)} %copy-done.3, f32[3,32,4,8,512]{4,3,2,1,0:T(8,128)S(1)} %bitcast.5, ...), custom_call_target="tpu_custom_call" | custom-call | tf_op jit(solution)/shard_map/finish/pallas_call | solution.py:472
  135.7 4.6 %broadcast_multiply_fusion = f32[4,768,768]{2,1,0:T(8,128)} fusion(f32[4,768,768]{2,1,0:T(8,128)S(1)} %get-tuple-element.10), kind=kLoop, calls=%fused_computation | loop fusion | flops 2359296 | bytes 18874368 | tf_op jit(solution)/shard_map/mul | solution.py:533
  140.4 0.1 fusion.4
  140.5 0.1 pad_maximum_fusion
  140.5 0.8 copy.17
  (5 shorter events, 0.1 us)
Async XLA Ops:
  1.8 1.9 %copy-start = (bf16[16,24,4096]{2,1,0:T(8,128)(2,1)S(1)}, bf16[16,24,4096]{2,1,0:T(8,128)(2,1)}, u32[]{:S(2)}) copy-start(bf16[16,24,4096]{2,1,0:T(8,128)(2,1)} %start.1) | copy-start | bytes 9437188
  3.7 0.9 copy-start.1
  4.7 0.9 copy-start.2
  5.6 0.7 copy-start.4
  107.2 0.7 copy-start.3

commit v6 on v5

--- a/solution.py
+++ b/solution.py
@@ -179,15 +179,21 @@
 
 def greet(wide, eight):
     barrier = pltpu.get_barrier_semaphore()
-    devices = lax.axis_size("wide") * lax.axis_size("eight")
+    groups, wides = lax.axis_size("eight"), lax.axis_size("wide")
+
+    def tell(to_wide, to_eight):
+        pl.semaphore_signal(barrier, inc=1, device_id=(to_wide, to_eight), device_id_type=MESH)
 
     def one(k, carry):
-        to = partner(k, wide, eight)
-        pl.semaphore_signal(barrier, inc=1, device_id=to, device_id_type=MESH)
-        return carry
-
-    lax.fori_loop(1, devices, one, 0)
-    return lambda: pl.semaphore_wait(barrier, devices - 1)
+        to_wide = (wide + k) & 31
+        for to_eight in range(groups):
+            tell(to_wide, to_eight)
+        return carry
+
+    lax.fori_loop(1, wides, one, 0)
+    for k in range(1, groups):
+        tell(wide, (eight + k) & 3)
+    return lambda: pl.semaphore_wait(barrier, groups * wides - 1)
 
 
 def all_of(ref):

time: 142 us -> 138 us (0.972)
  Pallas kernels: 128 us -> 124 us
    pallas_call x1, Pallas kernels: 27.8 us -> 25.1 us  [finished(): pl.pallas_call(finish_kernel, in_specs=[smem] * 3 + [vmem] * 3, out_specs...]
where the time goes in v6:
time: 138 us
  Pallas kernels  124 us (90%)
  local copies, waits for them, and re-layouts  7.08 us (5%)
  other arithmetic  5.61 us (4%)
    pallas_call x1, Pallas kernels, exchanged(): pl.pallas_call(exchange_kernel, in_specs=[pl.BlockSpec(memory_space=pltpu...  99.2 us
    pallas_call x1, Pallas kernels, finished(): pl.pallas_call(finish_kernel, in_specs=[smem] * 3 + [vmem] * 3, out_specs...  25.1 us
    unnamed x11, local copies, waits for them, and re-layouts  5.86 us
    mul x1, other arithmetic, body(): galerkin = galerkin * (1.0 / ECELLS)  4.64 us

profile of v6, /device:TPU:0, one launch (start us, length us, event | category | flops | bytes accessed | tf_op | source)
XLA Modules:
  0.0 137.6 jit_solution(16936937137605333872)
XLA Ops:
  0.6 0.7 add_select_fusion.1
  1.3 0.1 copy.14
  1.4 0.1 eq.34.dest
  1.5 0.1 copy.15
  1.6 0.1 reshape.43
  1.7 0.1 select_reduce_fusion
  1.8 0.0 copy-start
  1.8 1.9 %copy-done = bf16[16,24,4096]{2,1,0:T(8,128)(2,1)S(1)} copy-done((bf16[16,24,4096]{2,1,0:T(8,128)(2,1)S(1)}, bf16[16,24,4096]{2,1,0:T(8,128)(2,1)}, u32[]{:S(2)}) %copy-start) | copy-done | bytes 3145752
  3.7 0.0 copy-start.1
  3.7 0.9 copy-done.1
  4.7 0.0 copy-start.2
  4.7 0.9 copy-done.2
  5.6 0.0 copy-start.4
  5.6 0.7 copy-done.4
  6.2 99.2 %exchange.1 = (f32[3,128,8,512]{3,2,1,0:T(8,128)S(1)}, f32[128,12,128]{2,1,0:T(8,128)S(1)}, s32[32,8,128]{2,1,0:T(8,128)S(1)}) custom-call(s32[128]{0:T(128)S(1)} %get-tuple-element.21.order, s32[16]{0:T(128)S(1)} %copy-done.4, bf16[16,24,4096]{2,1,0:T(8,128)(2,1)S(1)} %copy-done, f32[16,4096]{1,0:T(8,128)S(1)} %copy-done.1, f32[4,64,96]{2,1,0:T(8,128)S(1)} %bitcast.7, ...), custom_call_target="tpu_custom_call" | custom-call | tf_op jit(solution)/shard_map/exchange/pallas_call | solution.py:327
  105.4 0.7 dynamic-slice_reduce_fusion.places
  106.1 0.1 select_reduce_fusion.1.where
  106.2 0.0 copy-start.3
  106.3 0.7 copy-done.3
  107.0 25.1 %finish.1 = (f32[4,768,768]{2,1,0:T(8,128)S(1)}, f32[4,4,12,128]{3,2,1,0:T(8,128)S(1)}) custom-call(s32[32]{0:T(128)S(1)} %select_reduce_fusion.1.where, s32[32]{0:T(128)S(1)} %dynamic-slice_reduce_fusion.places, s32[128]{0:T(128)S(1)} %eq.34.dest, f32[4,512]{1,0:T(4,128)S(1)} %copy-done.3, f32[3,32,4,8,512]{4,3,2,1,0:T(8,128)S(1)} %bitcast.5, ...), custom_call_target="tpu_custom_call" | custom-call | tf_op jit(solution)/shard_map/finish/pallas_call | solution.py:478
  132.0 4.6 %broadcast_multiply_fusion = f32[4,768,768]{2,1,0:T(8,128)} fusion(f32[4,768,768]{2,1,0:T(8,128)S(1)} %get-tuple-element.10), kind=kLoop, calls=%fused_computation | loop fusion | flops 2359296 | bytes 18874368 | tf_op jit(solution)/shard_map/mul | solution.py:539
  136.7 0.1 fusion.4
  136.8 0.1 pad_maximum_fusion
  136.9 0.8 copy.17
  (5 shorter events, 0.1 us)
Async XLA Ops:
  1.8 1.9 %copy-start = (bf16[16,24,4096]{2,1,0:T(8,128)(2,1)S(1)}, bf16[16,24,4096]{2,1,0:T(8,128)(2,1)}, u32[]{:S(2)}) copy-start(bf16[16,24,4096]{2,1,0:T(8,128)(2,1)} %start.1) | copy-start | bytes 9437188
  3.7 0.9 copy-start.1
  4.7 0.9 copy-start.2
  5.6 0.7 copy-start.4
  106.2 0.7 copy-start.3
